TPU v7x, 32 devices: a whole 2x2x4 slice. The times are simulated.
32 devices in a mesh: gx: 4 (over y, x), gy: 8 (over z, core).
Axes of the slice: x: 2, y: 2, z: 4, core: 2. Of those that a mesh axis runs over, the one named last changes fastest.
Arguments:
- e_field: float32 [3, 32, 256, 512], P(None, 'gx', 'gy'), may hold values from -6 to 6
- h_field: float32 [3, 32, 256, 512], P(None, 'gx', 'gy'), may hold values from -6 to 6
- polar: float32 [3, 32, 256, 512], P(None, 'gx', 'gy'), may hold values from -6 to 6
- polar_prev: float32 [3, 32, 256, 512], P(None, 'gx', 'gy'), may hold values from -6 to 6
- material: int32 [32, 256, 512], P('gx', 'gy'), may hold values from 0 to 3
- eps_table: float32 [4], replicated, may hold values from 1 to 6
- delta_table: float32 [4], replicated, may hold values from 0.5 to 4
- omega_table: float32 [4], replicated, may hold values from 0.2 to 1.2
- damping_table: float32 [4], replicated, may hold values from 0.02 to 0.6
- surface_flags: int32 [4, 8], P('gx', 'gy'), may hold values 0 or 1
Outputs:
- e_out: float32 [3, 32, 256, 512], P(None, 'gx', 'gy')
- h_out: float32 [3, 32, 256, 512], P(None, 'gx', 'gy')
- polar_out: float32 [3, 32, 256, 512], P(None, 'gx', 'gy')
- far_field: float32 [2, 2, 4, 16384], replicated
All inputs are finite; a program needn't handle non-finite values. No bound on the sum of `surface_flags` on one device may be relied on, other than what follows from the above.
Results may differ from a plain program's by a relative error of at most 0.0003.
Values sent between devices are 32-bit elements; how exact they have to be, the bound alone decides.
A program may use at most 256 MiB of HBM per device.

v0:
```python
import functools
import math

import jax
import jax.numpy as jnp
import numpy as np
from jax import lax
from jax.experimental import pallas as pl
from jax.experimental.pallas import tpu as pltpu
from jax.sharding import PartitionSpec as P

NTH = 64
NPH = 256
NDIR = 16384
ZS = 384
DT = 0.55
WAVELENGTHS = (5.0, 4.0)
MESH = pl.DeviceIdType.MESH
F32 = jnp.float32
BF16 = jnp.bfloat16
BY = 8


def coefficients(nmat, nz, eps, delta, omega, damping):
    coef = []
    for m in range(nmat):
        half = jnp.full((1, nz), damping[m], F32) * (DT / 2.0)
        denom = 1.0 + half
        om = jnp.full((1, nz), omega[m], F32)
        square = om * om * (DT * DT)
        coef.append((
            (2.0 - square) / denom,
            (half - 1.0) / denom,
            jnp.full((1, nz), delta[m], F32) * square / denom,
            1.0 / jnp.full((1, nz), eps[m], F32),
        ))
    return coef


def step_kernel(
    ngx, ngy, nmat,
    e_in, h_in, p_in, q_in, m_in, eps_in, delta_in, omega_in, damping_in, flags_in,
    e_out, h_out, p_out, g_out,
    E, H, PA, PB, MAT, ystage, ye, yh, gather, G, eps, delta, omega, damping, flags,
    in_sem, out_sem, xs_sem, xr_sem, ys_sem, yr_sem, g1s, g1r, g2s, g2r,
):
    cx, cy, nz = MAT.shape
    width = G.shape[2]
    gx = lax.axis_index("gx")
    gy = lax.axis_index("gy")

    loads = [
        pltpu.make_async_copy(e_in, E.at[:, pl.ds(0, cx)], in_sem.at[0]),
        pltpu.make_async_copy(h_in, H.at[:, pl.ds(1, cx)], in_sem.at[1]),
        pltpu.make_async_copy(p_in, PA, in_sem.at[2]),
        pltpu.make_async_copy(q_in, PB, in_sem.at[3]),
        pltpu.make_async_copy(m_in, MAT, in_sem.at[4]),
        pltpu.make_async_copy(eps_in, eps, in_sem.at[5]),
        pltpu.make_async_copy(delta_in, delta, in_sem.at[6]),
        pltpu.make_async_copy(omega_in, omega, in_sem.at[7]),
        pltpu.make_async_copy(damping_in, damping, in_sem.at[8]),
        pltpu.make_async_copy(flags_in, flags, in_sem.at[9]),
    ]
    for load in loads:
        load.start()

    barrier = pltpu.get_barrier_semaphore()
    for k in range(1, ngx):
        pl.semaphore_signal(barrier, inc=1, device_id=(lax.rem(gx + k, ngx), gy), device_id_type=MESH)
    for k in range(1, ngy):
        pl.semaphore_signal(barrier, inc=1, device_id=(gx, lax.rem(gy + k, ngy)), device_id_type=MESH)

    @pl.when(gx == ngx - 1)
    def _():
        for c in (1, 2):
            E[c, cx] = jnp.zeros((cy, nz), F32)

    @pl.when(gx == 0)
    def _():
        for c in (1, 2):
            H[c, 0] = jnp.zeros((cy, nz), F32)

    @pl.when(gy == ngy - 1)
    def _():
        ye[...] = jnp.zeros(ye.shape, F32)

    @pl.when(gy == 0)
    def _():
        yh[...] = jnp.zeros(yh.shape, F32)

    def copies(rnd, step):
        if rnd % 2 == 0:
            field, at_src, at_dst, ydst = E, 0, cx, ye.at[step]
            tx, ty = gx - 1, gy - 1
            sends_x, sends_y = gx > 0, gy > 0
            takes_x, takes_y = gx < ngx - 1, gy < ngy - 1
        else:
            field, at_src, at_dst, ydst = H, cx, 0, yh.at[step]
            tx, ty = gx + 1, gy + 1
            sends_x, sends_y = gx < ngx - 1, gy < ngy - 1
            takes_x, takes_y = gx > 0, gy > 0
        xcopies = []
        for i in range(2 * (cy // BY)):
            c, y = 1 + i % 2, (i // 2) * BY
            xcopies.append(pltpu.make_async_remote_copy(
                src_ref=field.at[c, at_src, pl.ds(y, BY)], dst_ref=field.at[c, at_dst, pl.ds(y, BY)],
                send_sem=xs_sem.at[rnd, i], recv_sem=xr_sem.at[rnd, i],
                device_id=(lax.rem(tx + ngx, ngx), gy), device_id_type=MESH))
        ycopy = pltpu.make_async_remote_copy(
            src_ref=ystage.at[rnd], dst_ref=ydst, send_sem=ys_sem.at[rnd], recv_sem=yr_sem.at[rnd],
            device_id=(gx, lax.rem(ty + ngy, ngy)), device_id_type=MESH)
        return xcopies, ycopy, sends_x, sends_y, takes_x, takes_y

    def send_x(rnd, step, block):
        xcopies, _, sends_x, _, _, _ = copies(rnd, step)

        @pl.when(sends_x)
        def _():
            for xcopy in xcopies[2 * block : 2 * block + 2]:
                xcopy.start()

    def send_y(rnd, step):
        _, ycopy, _, sends_y, _, _ = copies(rnd, step)
        for i, c in enumerate((0, 2)):
            for x in range(cx):
                if rnd % 2 == 0:
                    ystage[rnd, i, x : x + 1, :] = E[c, x, 0:1, :]
                else:
                    ystage[rnd, i, x : x + 1, :] = H[c, x + 1, cy - 1 : cy, :]
        pl.when(sends_y)(ycopy.start)

    def take_x(rnd, step, block):
        xcopies, _, _, _, takes_x, _ = copies(rnd, step)

        @pl.when(takes_x)
        def _():
            for xcopy in xcopies[2 * block : 2 * block + 2]:
                xcopy.wait_recv()

    def take_y(rnd, step):
        _, ycopy, _, _, _, takes_y = copies(rnd, step)
        pl.when(takes_y)(ycopy.wait_recv)

    def sent_x(rnd, step):
        xcopies, _, sends_x, _, _, _ = copies(rnd, step)

        @pl.when(sends_x)
        def _():
            for xcopy in xcopies:
                xcopy.wait_send()

    def sent_y(rnd, step):
        _, ycopy, _, sends_y, _, _ = copies(rnd, step)
        pl.when(sends_y)(ycopy.wait_send)

    row_id = lax.broadcasted_iota(jnp.int32, (BY, nz), 0)
    lane_id = lax.broadcasted_iota(jnp.int32, (BY, nz), 1)

    def up_y(v, row):
        return jnp.where(row_id == BY - 1, row, pltpu.roll(v, BY - 1, 0))

    def up_z(v):
        return jnp.where(lane_id == nz - 1, 0.0, pltpu.roll(v, nz - 1, 1))

    def down_y(v, row):
        return jnp.where(row_id == 0, row, pltpu.roll(v, 1, 0))

    def down_z(v):
        return jnp.where(lane_id == 0, 0.0, pltpu.roll(v, 1, 1))

    def h_plane(step, x, blocks):
        for y in [BY * block for block in blocks]:
            here = pl.ds(y, BY)
            ex, ey, ez = E[0, x, here, :], E[1, x, here, :], E[2, x, here, :]
            if y + BY < cy:
                rx, rz = E[0, x, y + BY : y + BY + 1, :], E[2, x, y + BY : y + BY + 1, :]
            else:
                rx, rz = ye[step, 0, pl.ds(x, 1), :], ye[step, 1, pl.ds(x, 1), :]
            eyx, ezx = E[1, x + 1, here, :], E[2, x + 1, here, :]
            curl_x = (up_y(ez, rz) - ez) - (up_z(ey) - ey)
            curl_y = (up_z(ex) - ex) - (ezx - ez)
            curl_z = (eyx - ey) - (up_y(ex, rx) - ex)
            H[0, x + 1, here, :] = H[0, x + 1, here, :] - DT * curl_x
            H[1, x + 1, here, :] = H[1, x + 1, here, :] - DT * curl_y
            H[2, x + 1, here, :] = H[2, x + 1, here, :] - DT * curl_z

    def e_plane(step, x, coef, blocks):
        now, old = (PA, PB) if step == 0 else (PB, PA)
        for y in [BY * block for block in blocks]:
            here = pl.ds(y, BY)
            mat = MAT[x, here, :]
            vox = [jnp.broadcast_to(coef[nmat - 1][i], (BY, nz)) for i in range(4)]
            for m in range(nmat - 1):
                hit = mat == m
                vox = [jnp.where(hit, coef[m][i], vox[i]) for i in range(4)]
            a, b, c, inv = vox
            hx, hy, hz = H[0, x + 1, here, :], H[1, x + 1, here, :], H[2, x + 1, here, :]
            if y > 0:
                rx, rz = H[0, x + 1, y - 1 : y, :], H[2, x + 1, y - 1 : y, :]
            else:
                rx, rz = yh[step, 0, pl.ds(x, 1), :], yh[step, 1, pl.ds(x, 1), :]
            hyx, hzx = H[1, x, here, :], H[2, x, here, :]
            curls = (
                (hz - down_y(hz, rz)) - (hy - down_z(hy)),
                (hx - down_z(hx)) - (hz - hzx),
                (hy - hyx) - (hx - down_y(hx, rx)),
            )
            for i in range(3):
                e, p = E[i, x, here, :], now[i, x, here, :]
                new = a * p + b * old[i, x, here, :] + c * e
                E[i, x, here, :] = e + (DT * curls[i] - (new - p)) * inv
                old[i, x, here, :] = new

    surf_lane = lax.broadcasted_iota(jnp.int32, (cy, width), 1)

    def surface(step, flag):
        def body(x, acc):
            base = (gx * cx + x) * 4
            cols = (
                -H[1, x + 1, :, ZS : ZS + 1], H[0, x + 1, :, ZS : ZS + 1],
                E[1, x, :, ZS : ZS + 1], -E[0, x, :, ZS : ZS + 1],
            )
            for j in range(4):
                acc = jnp.where(surf_lane == base + j, cols[j] * flag, acc)
            return acc

        gather[step, gx] = lax.fori_loop(0, cx, body, jnp.zeros((cy, width), F32))

    def first(step, k):
        return pltpu.make_async_remote_copy(
            src_ref=gather.at[step, gx], dst_ref=gather.at[step, gx],
            send_sem=g1s.at[step, k], recv_sem=g1r.at[step, k],
            device_id=(lax.rem(gx + k, ngx), gy), device_id_type=MESH)

    def second(step, k):
        rows = pl.ds(pl.multiple_of(gy * cy, cy), cy)
        return pltpu.make_async_remote_copy(
            src_ref=G.at[step, rows], dst_ref=G.at[step, rows],
            send_sem=g2s.at[step, k], recv_sem=g2r.at[step, k],
            device_id=(gx, lax.rem(gy + k, ngy)), device_id_type=MESH)

    def gather_first(step):
        for k in range(1, ngx):
            first(step, k).start()

    def gather_second(step):
        for k in range(1, ngx):
            first(step, k).wait()
        total = gather[step, 0]
        for i in range(1, ngx):
            total = total + gather[step, i]
        G[step, pl.ds(pl.multiple_of(gy * cy, cy), cy)] = total
        for k in range(1, ngy):
            second(step, k).start()

    def gather_end(step):
        for k in range(1, ngy):
            second(step, k).wait()

    loads[0].wait()
    pl.semaphore_wait(barrier, ngx + ngy - 2)
    blocks = range(cy // BY)
    send_y(0, 0)
    for block in blocks:
        send_x(0, 0, block)
    for load in loads[1:2] + loads[5:]:
        load.wait()

    coef = coefficients(nmat, nz, eps, delta, omega, damping)
    flag = flags[0, 0].astype(F32)

    for step in range(2):
        down, up = 2 * step, 2 * step + 1
        take_y(down, step)

        @pl.loop(0, cx - 1)
        def _(x):
            h_plane(step, x, blocks)

        for block in blocks:
            take_x(down, step, block)
            h_plane(step, cx - 1, [block])
            send_x(up, step, block)
        send_y(up, step)
        if step == 0:
            for load in loads[2:5]:
                load.wait()
        else:
            pltpu.make_async_copy(H.at[:, pl.ds(1, cx)], h_out, out_sem.at[0]).start()
            gather_second(0)
        sent_x(down, step)
        take_y(up, step)

        @pl.loop(1, cx)
        def _(x):
            e_plane(step, x, coef, blocks)

        for block in blocks:
            take_x(up, step, block)
            e_plane(step, 0, coef, [block])
            if step == 0:
                send_x(2, 1, block)
        if step == 0:
            send_y(2, 1)
            sent_x(up, step)
        surface(step, flag)
        gather_first(step)

    saves = [
        pltpu.make_async_copy(H.at[:, pl.ds(1, cx)], h_out, out_sem.at[0]),
        pltpu.make_async_copy(E.at[:, pl.ds(0, cx)], e_out, out_sem.at[1]),
        pltpu.make_async_copy(PA, p_out, out_sem.at[2]),
    ]
    saves[1].start()
    saves[2].start()
    gather_end(0)
    gather_second(1)
    gather_end(1)
    last = pltpu.make_async_copy(G, g_out, out_sem.at[3])
    last.start()
    sent_x(3, 1)
    for rnd in range(4):
        sent_y(rnd, rnd // 2)
    for save in saves:
        save.wait()
    last.wait()


def make_seeds():
    theta = (np.arange(NTH, dtype=np.float64)[:, None] + 0.5) * (math.pi / 2.0 / NTH)
    phi = (np.arange(NPH // 4, dtype=np.float64)[None, :] + 0.5) * (2.0 * math.pi / NPH)
    ux = (np.sin(theta) * np.cos(phi)).reshape(-1)
    uy = (np.sin(theta) * np.sin(phi)).reshape(-1)
    rows = []
    for length in WAVELENGTHS:
        wave = 2.0 * math.pi / length
        for angle in (uy, 8.0 * uy, ux, 2.0 * ux):
            rows += [np.cos(wave * angle), np.sin(wave * angle)]
    return np.stack(rows).astype(np.float32).reshape(16, -1, TILE).swapaxes(0, 1).copy()


def make_spread():
    spread = np.zeros((256, 256), np.float32)
    for r in range(256):
        t, p = (r % 128) // 64, r % 64
        spread[r, t * 128 + (p if r < 128 else 127 - p)] = 1.0
    return spread


TILE = 512


def far_kernel(
    nx, ny, g_ref, seeds, spread, e_in, h_in, p_in, far, e_out, h_out, p_out,
    a_wide, a_low, t_cos, t_sin, s_cos, s_sin, packed, e_pass, h_pass, p_pass, sem,
):
    pid = pl.program_id(0)
    width = 4 * nx
    tile = pl.num_programs(0) * lax.rem(lax.axis_index("gy"), 2) + pid
    fields = enumerate(zip((e_in, h_in, p_in), (e_pass, h_pass, p_pass), (e_out, h_out, p_out)))
    moves = [
        (pltpu.make_async_copy(src, mid, sem.at[0, i]), pltpu.make_async_copy(mid, dst, sem.at[1, i]))
        for i, (src, mid, dst) in fields
    ]

    @pl.when(pid == 0)
    def _():
        for load, _ in moves:
            load.start()
        for s in range(2):
            a = g_ref[s].T
            high = a.astype(BF16)
            rows = pl.ds(s * width, width)
            a_wide[rows, 0:ny] = high
            a_wide[rows, ny : 2 * ny] = high
            a_low[rows, :] = (a - high.astype(F32)).astype(BF16)

    @pl.when(pid == 1)
    def _():
        for load, save in moves:
            load.wait()
            save.start()

    scale = 1.0 / math.sqrt(nx * ny)
    part = 256
    sub = lax.broadcasted_iota(jnp.int32, (8, part), 0)
    for f in range(2):
        omega = 2.0 * math.pi / WAVELENGTHS[f]
        kappa = [math.cos(omega * (s + 1) * DT) * scale for s in range(2)]
        sigma = [math.sin(omega * (s + 1) * DT) * scale for s in range(2)]

        def seed(i, lanes):
            row = 8 * f + i
            return jnp.broadcast_to(seeds[tile, row : row + 1, lanes], (8, part))

        def times(a, b):
            return (a[0] * b[0] - a[1] * b[1], a[0] * b[1] + a[1] * b[0])

        one = jnp.ones((8, part), F32)
        zero = jnp.zeros((8, part), F32)

        def chosen(bit, z):
            on = (sub & bit) != 0
            return (jnp.where(on, z[0], one), jnp.where(on, z[1], zero))

        for o in range(0, TILE, part):
            lanes = slice(o, o + part)
            e1 = (seed(0, lanes), seed(1, lanes))
            e8 = (seed(2, lanes), seed(3, lanes))
            e2 = times(e1, e1)
            e4 = times(e2, e2)
            v = times(times(chosen(1, e1), chosen(2, e2)), chosen(4, e4))
            e16 = times(e8, e8)
            w = times(v, e8)

            def fill(k, carry):
                v, w = (carry[0], carry[1]), (carry[2], carry[3])
                at = pl.multiple_of(k * 16, 16)
                for i, table in ((0, t_cos), (1, t_sin)):
                    full = jnp.concatenate([v[i], w[i]], axis=0)
                    high = full.astype(BF16)
                    table[pl.ds(at, 16), lanes] = high
                    table[pl.ds(pl.multiple_of(at + ny, 16), 16), lanes] = (full - high.astype(F32)).astype(BF16)
                return times(v, e16) + times(w, e16)

            lax.fori_loop(0, ny // 16, fill, v + w, unroll=16)

        for table, result in ((t_cos, s_cos), (t_sin, s_sin)):
            result[...] = jnp.dot(a_wide[...], table[...], preferred_element_type=F32) + jnp.dot(
                a_low[...], table[0:ny, :], preferred_element_type=F32)

        for o in range(0, TILE, part):
            lanes = slice(o, o + part)
            w0 = chosen(4, (seed(4, lanes), seed(5, lanes)))
            e2 = (seed(6, lanes), seed(7, lanes))

            def add(k, carry):
                w, sums = (carry[0], carry[1]), carry[2:]
                fresh = []
                for s in range(2):
                    rows = pl.ds(pl.multiple_of(s * width + k * 8, 8), 8)
                    c, d = s_cos[rows, lanes], s_sin[rows, lanes]
                    fresh += [c * w[0], c * w[1], d * w[0], d * w[1]]
                return times(w, e2) + tuple(t + n for t, n in zip(sums, fresh))

            out = lax.fori_loop(0, nx // 2, add, w0 + (zero,) * 8, unroll=16)
            sums = out[2:]
            re = [zero] * 4
            im = [zero] * 4
            for s in range(2):
                cc, cs, sc, ss = sums[4 * s : 4 * s + 4]
                a, b, c, d = cc - ss, cs + sc, cc + ss, sc - cs
                k, g = kappa[s], sigma[s]
                re[0] += a * k + b * g
                im[0] += b * k - a * g
                re[1] += c * k + d * g
                im[1] += d * k - c * g
                re[2] += a * k - b * g
                im[2] -= b * k + a * g
                re[3] += c * k - d * g
                im[3] -= d * k + c * g
            for q in range(4):
                r = re[q] + pltpu.roll(re[q], 4, 0)
                i = im[q] + pltpu.roll(im[q], 4, 0)
                both = jnp.where(sub < 4, r, i)
                for pair in range(part // 128):
                    at = (((o // 128 + pair) * 2 + f) * 2 + q // 2) * 8
                    packed[at : at + 8, (q % 2) * 128 : (q % 2) * 128 + 128] = both[:, pair * 128 : pair * 128 + 128]

    done = jnp.dot(packed[...], spread[...], precision=lax.Precision.HIGHEST, preferred_element_type=F32)
    for pair in range(TILE // 128):
        for f in range(2):
            for h in range(2):
                at = ((pair * 2 + f) * 2 + h) * 8
                for t in range(2):
                    d = (2 * pair + t) * 256 + h * 128
                    far[f, 0, :, d : d + 128] = done[at : at + 4, t * 128 : t * 128 + 128]
                    far[f, 1, :, d : d + 128] = done[at + 4 : at + 8, t * 128 : t * 128 + 128]

    @pl.when(pid == pl.num_programs(0) - 1)
    def _():
        for _, save in moves:
            save.wait()


def share_kernel(half, far, slots, sem):
    gx, gy = lax.axis_index("gx"), lax.axis_index("gy")
    core = lax.rem(gy, 2)
    other = (gx, gy + 1 - 2 * core)
    count = half.shape[3]
    barrier = pltpu.get_barrier_semaphore()
    pl.semaphore_signal(barrier, inc=1, device_id=other, device_id_type=MESH)
    pl.semaphore_wait(barrier, 1)
    sends = []
    for i in range(4):
        f, r = i // 2, i % 2
        send = pltpu.make_async_remote_copy(
            src_ref=half.at[f, r], dst_ref=slots.at[f, r], send_sem=sem.at[0, i], recv_sem=sem.at[1, i],
            device_id=other, device_id_type=MESH)
        send.start()
        sends.append(send)
    mine = pl.ds(pl.multiple_of(core * count, count), count)
    theirs = pl.ds(pl.multiple_of((1 - core) * count, count), count)
    far[:, :, :, mine] = half[...]
    for i, send in enumerate(sends):
        f, r = i // 2, i % 2
        send.wait()
        far[f, r, :, theirs] = slots[f, r]


def shards(
    e_field, h_field, polar, polar_prev, material,
    eps_table, delta_table, omega_table, damping_table, surface_flags,
):
    _, cx, cy, nz = e_field.shape
    ngx, ngy = lax.axis_size("gx"), lax.axis_size("gy")
    nx, ny = ngx * cx, ngy * cy
    width = 4 * nx
    hbm = pl.BlockSpec(memory_space=pl.ANY)
    field = jax.ShapeDtypeStruct(e_field.shape, F32)
    dma = pltpu.SemaphoreType.DMA
    e, h, p, g = pl.pallas_call(
        functools.partial(step_kernel, ngx, ngy, eps_table.shape[0]),
        out_shape=(field, field, field, jax.ShapeDtypeStruct((2, ny, width), F32)),
        in_specs=[hbm] * 10,
        out_specs=(hbm,) * 4,
        scratch_shapes=[
            pltpu.VMEM((3, cx + 1, cy, nz), F32),
            pltpu.VMEM((3, cx + 1, cy, nz), F32),
            pltpu.VMEM((3, cx, cy, nz), F32),
            pltpu.VMEM((3, cx, cy, nz), F32),
            pltpu.VMEM((cx, cy, nz), jnp.int32),
            pltpu.VMEM((4, 2, cx, nz), F32),
            pltpu.VMEM((2, 2, cx, nz), F32),
            pltpu.VMEM((2, 2, cx, nz), F32),
            pltpu.VMEM((2, ngx, cy, width), F32),
            pltpu.VMEM((2, ny, width), F32),
            *[pltpu.SMEM(table.shape, F32) for table in (eps_table, delta_table, omega_table, damping_table)],
            pltpu.SMEM(surface_flags.shape, jnp.int32),
            dma((10,)), dma((4,)), dma((4, 2 * (cy // BY))), dma((4, 2 * (cy // BY))), dma((4,)), dma((4,)),
            dma((2, ngx)), dma((2, ngx)), dma((2, ngy)), dma((2, ngy)),
        ],
        compiler_params=pltpu.CompilerParams(
            collective_id=0, has_side_effects=True, vmem_limit_bytes=58 * 1024 * 1024),
    )(e_field, h_field, polar, polar_prev, material,
      eps_table, delta_table, omega_table, damping_table, surface_flags)

    steps = (NDIR // 4) // TILE // 2
    whole = lambda *shape: pl.BlockSpec(shape, lambda i: (0,) * len(shape))
    far, e, h, p = pl.pallas_call(
        functools.partial(far_kernel, nx, ny),
        grid=(steps,),
        out_shape=(jax.ShapeDtypeStruct((2, 2, 4, NDIR // 2), F32), field, field, field),
        in_specs=[
            whole(2, ny, width),
            whole(2 * steps, 16, TILE),
            whole(256, 256),
            hbm, hbm, hbm,
        ],
        out_specs=(pl.BlockSpec((2, 2, 4, 4 * TILE), lambda i: (0, 0, 0, i)), hbm, hbm, hbm),
        scratch_shapes=[
            pltpu.VMEM((2 * width, 2 * ny), BF16),
            pltpu.VMEM((2 * width, ny), BF16),
            pltpu.VMEM((2 * ny, TILE), BF16),
            pltpu.VMEM((2 * ny, TILE), BF16),
            pltpu.VMEM((2 * width, TILE), F32),
            pltpu.VMEM((2 * width, TILE), F32),
            pltpu.VMEM((4 * (TILE // 128) * 8, 256), F32),
            *[pltpu.VMEM(e_field.shape, F32)] * 3,
            dma((2, 3)),
        ],
        compiler_params=pltpu.CompilerParams(vmem_limit_bytes=56 * 1024 * 1024),
    )(g, jnp.asarray(make_seeds()), jnp.asarray(make_spread()), e, h, p)
    far = pl.pallas_call(
        share_kernel,
        out_shape=jax.ShapeDtypeStruct((2, 2, 4, NDIR), F32),
        in_specs=[pl.BlockSpec(memory_space=pltpu.VMEM)],
        out_specs=pl.BlockSpec(memory_space=pltpu.VMEM),
        scratch_shapes=[pltpu.VMEM((2, 2, 4, NDIR // 2), F32), dma((2, 4))],
        compiler_params=pltpu.CompilerParams(
            collective_id=1, has_side_effects=True, vmem_limit_bytes=56 * 1024 * 1024),
    )(far)
    return e, h, p, far


def solution(mesh):
    cells = P(None, "gx", "gy", None)
    placed = (cells, cells, cells, cells, P("gx", "gy", None), P(), P(), P(), P(), P("gx", "gy"))
    return jax.shard_map(
        shards, mesh=mesh, in_specs=placed, out_specs=(cells, cells, cells, P()), check_vma=False,
    )
```

profile of v0, /device:TPU:0, one launch (start us, length us, event | category | flops | bytes accessed | tf_op | source)
XLA Modules:
  0.0 48.3 jit_solution(14326738644145518325)
XLA Ops:
  1.3 31.5 %shard_map.147 = (f32[3,8,32,512]{3,2,1,0:T(8,128)}, f32[3,8,32,512]{3,2,1,0:T(8,128)}, f32[3,8,32,512]{3,2,1,0:T(8,128)}, f32[2,256,128]{2,1,0:T(8,128)}) custom-call(f32[3,8,32,512]{3,2,1,0:T(8,128)} %e_in.1, f32[3,8,32,512]{3,2,1,0:T(8,128)} %h_in.1, f32[3,8,32,512]{3,2,1,0:T(8,128)} %p_in.1, f32[3,8,32,512]{3,2,1,0:T(8,128)} %q_in.1, ...), custom_call_target="tpu_custom_call" | custom-call | tf_op jit(solution)/shard_map/pallas_call | solution.py:522
  32.8 9.2 %shard_map.148 = (f32[2,2,4,8192]{3,2,1,0:T(4,128)}, f32[3,8,32,512]{3,2,1,0:T(8,128)}, f32[3,8,32,512]{3,2,1,0:T(8,128)}, f32[3,8,32,512]{3,2,1,0:T(8,128)}) custom-call(f32[2,256,128]{2,1,0:T(8,128)} %get-tuple-element.12.g_ref, f32[8,16,512]{2,1,0:T(8,128)} %constant.4.clone.seeds, f32[256,256]{1,0:T(8,128)} %constant.5.clone.spread, ...), custom_call_target="tpu_custom_call" | custom-call | tf_op jit(solution)/shard_map/pallas_call | solution.py:550
  42.0 4.0 %shard_map.149 = f32[2,2,4,16384]{3,2,1,0:T(4,128)} custom-call(f32[2,2,4,8192]{3,2,1,0:T(4,128)} %get-tuple-element.19.half), custom_call_target="tpu_custom_call" | custom-call | tf_op jit(solution)/shard_map/pallas_call | solution.py:574
  46.0 2.3 %copy.18 = f32[2,2,4,16384]{3,2,1,0:T(4,128)} copy(f32[2,2,4,16384]{3,2,1,0:T(4,128)} %shard_map.149) | data formatting | bytes 2097152
where the time goes:
time: 48.5 us; the launch traced here: 48.3 us
  Pallas kernels  44.7 us (92%)
  local copies, waits for them, and re-layouts  2.26 us (5%)
  between operations  1.3 us (3%)
    pallas_call x1, Pallas kernels, shards(): pl.pallas_call(functools.partial(step_kernel, ngx, ngy, eps_table.shape[0...  31.5 us
    pallas_call x1, Pallas kernels, shards(): pl.pallas_call(functools.partial(far_kernel, nx, ny), grid=(steps,), out_...  9.21 us
    pallas_call x1, Pallas kernels, shards(): pl.pallas_call(share_kernel, out_shape=jax.ShapeDtypeStruct((2, 2, 4, NDI...  4.02 us
    unnamed x1, local copies, waits for them, and re-layouts  2.26 us

commit v1 on v0

v1 whole, which is shorter than its diff:
```python
import functools
import math

import jax
import jax.numpy as jnp
import numpy as np
from jax import lax
from jax.experimental import pallas as pl
from jax.experimental.pallas import tpu as pltpu
from jax.sharding import PartitionSpec as P

NTH = 64
NPH = 256
NDIR = 16384
ZS = 384
DT = 0.55
WAVELENGTHS = (5.0, 4.0)
MESH = pl.DeviceIdType.MESH
F32 = jnp.float32
BF16 = jnp.bfloat16
BY = 8


def coefficients(nmat, nz, eps, delta, omega, damping):
    coef = []
    for m in range(nmat):
        half = jnp.full((1, nz), damping[m], F32) * (DT / 2.0)
        denom = 1.0 + half
        om = jnp.full((1, nz), omega[m], F32)
        square = om * om * (DT * DT)
        coef.append((
            (2.0 - square) / denom,
            (half - 1.0) / denom,
            jnp.full((1, nz), delta[m], F32) * square / denom,
            1.0 / jnp.full((1, nz), eps[m], F32),
        ))
    return coef


def step_kernel(
    ngx, ngy, nmat,
    e_in, h_in, p_in, q_in, m_in, eps_in, delta_in, omega_in, damping_in, flags_in,
    e_out, h_out, p_out, g_out,
    E, H, PA, PB, MAT, ystage, ye, yh, G, eps, delta, omega, damping, flags,
    in_sem, out_sem, xs_sem, xr_sem, ys_sem, yr_sem, g1s, g1r, all_in,
):
    cx, cy, nz = MAT.shape
    gx = lax.axis_index("gx")
    gy = lax.axis_index("gy")

    loads = [
        pltpu.make_async_copy(e_in, E.at[:, pl.ds(0, cx)], in_sem.at[0]),
        pltpu.make_async_copy(h_in, H.at[:, pl.ds(1, cx)], in_sem.at[1]),
        pltpu.make_async_copy(p_in, PA, in_sem.at[2]),
        pltpu.make_async_copy(q_in, PB, in_sem.at[3]),
        pltpu.make_async_copy(m_in, MAT, in_sem.at[4]),
        pltpu.make_async_copy(eps_in, eps, in_sem.at[5]),
        pltpu.make_async_copy(delta_in, delta, in_sem.at[6]),
        pltpu.make_async_copy(omega_in, omega, in_sem.at[7]),
        pltpu.make_async_copy(damping_in, damping, in_sem.at[8]),
        pltpu.make_async_copy(flags_in, flags, in_sem.at[9]),
    ]
    for load in loads:
        load.start()

    barrier = pltpu.get_barrier_semaphore()
    for k in range(1, ngx):
        pl.semaphore_signal(barrier, inc=1, device_id=(lax.rem(gx + k, ngx), gy), device_id_type=MESH)
    for k in range(1, ngy):
        pl.semaphore_signal(barrier, inc=1, device_id=(gx, lax.rem(gy + k, ngy)), device_id_type=MESH)

    @pl.when(gx == ngx - 1)
    def _():
        for c in (1, 2):
            E[c, cx] = jnp.zeros((cy, nz), F32)

    @pl.when(gx == 0)
    def _():
        for c in (1, 2):
            H[c, 0] = jnp.zeros((cy, nz), F32)

    @pl.when(gy == ngy - 1)
    def _():
        ye[...] = jnp.zeros(ye.shape, F32)

    @pl.when(gy == 0)
    def _():
        yh[...] = jnp.zeros(yh.shape, F32)

    def copies(rnd, step):
        if rnd % 2 == 0:
            field, at_src, at_dst, ydst = E, 0, cx, ye.at[step]
            tx, ty = gx - 1, gy - 1
            sends_x, sends_y = gx > 0, gy > 0
            takes_x, takes_y = gx < ngx - 1, gy < ngy - 1
        else:
            field, at_src, at_dst, ydst = H, cx, 0, yh.at[step]
            tx, ty = gx + 1, gy + 1
            sends_x, sends_y = gx < ngx - 1, gy < ngy - 1
            takes_x, takes_y = gx > 0, gy > 0
        xcopies = []
        for i in range(2 * (cy // BY)):
            c, y = 1 + i % 2, (i // 2) * BY
            xcopies.append(pltpu.make_async_remote_copy(
                src_ref=field.at[c, at_src, pl.ds(y, BY)], dst_ref=field.at[c, at_dst, pl.ds(y, BY)],
                send_sem=xs_sem.at[rnd, i], recv_sem=xr_sem.at[rnd, i],
                device_id=(lax.rem(tx + ngx, ngx), gy), device_id_type=MESH))
        ycopy = pltpu.make_async_remote_copy(
            src_ref=ystage.at[rnd], dst_ref=ydst, send_sem=ys_sem.at[rnd], recv_sem=yr_sem.at[rnd],
            device_id=(gx, lax.rem(ty + ngy, ngy)), device_id_type=MESH)
        return xcopies, ycopy, sends_x, sends_y, takes_x, takes_y

    def send_x(rnd, step, block):
        xcopies, _, sends_x, _, _, _ = copies(rnd, step)

        @pl.when(sends_x)
        def _():
            for xcopy in xcopies[2 * block : 2 * block + 2]:
                xcopy.start()

    def send_y(rnd, step):
        _, ycopy, _, sends_y, _, _ = copies(rnd, step)
        for i, c in enumerate((0, 2)):
            for x in range(cx):
                if rnd % 2 == 0:
                    ystage[rnd, i, x : x + 1, :] = E[c, x, 0:1, :]
                else:
                    ystage[rnd, i, x : x + 1, :] = H[c, x + 1, cy - 1 : cy, :]
        pl.when(sends_y)(ycopy.start)

    def take_x(rnd, step, block):
        xcopies, _, _, _, takes_x, _ = copies(rnd, step)

        @pl.when(takes_x)
        def _():
            for xcopy in xcopies[2 * block : 2 * block + 2]:
                xcopy.wait_recv()

    def take_y(rnd, step):
        _, ycopy, _, _, _, takes_y = copies(rnd, step)
        pl.when(takes_y)(ycopy.wait_recv)

    def sent_x(rnd, step):
        xcopies, _, sends_x, _, _, _ = copies(rnd, step)

        @pl.when(sends_x)
        def _():
            for xcopy in xcopies:
                xcopy.wait_send()

    def sent_y(rnd, step):
        _, ycopy, _, sends_y, _, _ = copies(rnd, step)
        pl.when(sends_y)(ycopy.wait_send)

    row_id = lax.broadcasted_iota(jnp.int32, (BY, nz), 0)
    lane_id = lax.broadcasted_iota(jnp.int32, (BY, nz), 1)

    def up_y(v, row):
        return jnp.where(row_id == BY - 1, row, pltpu.roll(v, BY - 1, 0))

    def up_z(v):
        return jnp.where(lane_id == nz - 1, 0.0, pltpu.roll(v, nz - 1, 1))

    def down_y(v, row):
        return jnp.where(row_id == 0, row, pltpu.roll(v, 1, 0))

    def down_z(v):
        return jnp.where(lane_id == 0, 0.0, pltpu.roll(v, 1, 1))

    def h_plane(step, x, blocks):
        for y in [BY * block for block in blocks]:
            here = pl.ds(y, BY)
            ex, ey, ez = E[0, x, here, :], E[1, x, here, :], E[2, x, here, :]
            if y + BY < cy:
                rx, rz = E[0, x, y + BY : y + BY + 1, :], E[2, x, y + BY : y + BY + 1, :]
            else:
                rx, rz = ye[step, 0, pl.ds(x, 1), :], ye[step, 1, pl.ds(x, 1), :]
            eyx, ezx = E[1, x + 1, here, :], E[2, x + 1, here, :]
            curl_x = (up_y(ez, rz) - ez) - (up_z(ey) - ey)
            curl_y = (up_z(ex) - ex) - (ezx - ez)
            curl_z = (eyx - ey) - (up_y(ex, rx) - ex)
            H[0, x + 1, here, :] = H[0, x + 1, here, :] - DT * curl_x
            H[1, x + 1, here, :] = H[1, x + 1, here, :] - DT * curl_y
            H[2, x + 1, here, :] = H[2, x + 1, here, :] - DT * curl_z

    def e_plane(step, x, coef, blocks):
        now, old = (PA, PB) if step == 0 else (PB, PA)
        for y in [BY * block for block in blocks]:
            here = pl.ds(y, BY)
            mat = MAT[x, here, :]
            vox = [jnp.broadcast_to(coef[nmat - 1][i], (BY, nz)) for i in range(4)]
            for m in range(nmat - 1):
                hit = mat == m
                vox = [jnp.where(hit, coef[m][i], vox[i]) for i in range(4)]
            a, b, c, inv = vox
            hx, hy, hz = H[0, x + 1, here, :], H[1, x + 1, here, :], H[2, x + 1, here, :]
            if y > 0:
                rx, rz = H[0, x + 1, y - 1 : y, :], H[2, x + 1, y - 1 : y, :]
            else:
                rx, rz = yh[step, 0, pl.ds(x, 1), :], yh[step, 1, pl.ds(x, 1), :]
            hyx, hzx = H[1, x, here, :], H[2, x, here, :]
            curls = (
                (hz - down_y(hz, rz)) - (hy - down_z(hy)),
                (hx - down_z(hx)) - (hz - hzx),
                (hy - hyx) - (hx - down_y(hx, rx)),
            )
            for i in range(3):
                e, p = E[i, x, here, :], now[i, x, here, :]
                new = a * p + b * old[i, x, here, :] + c * e
                E[i, x, here, :] = e + (DT * curls[i] - (new - p)) * inv
                old[i, x, here, :] = new

    me = gx * ngy + gy
    count = ngx * ngy
    turn_x, turn_y = 2 * gx >= ngx, 2 * gy >= ngy
    tile_lane = lax.broadcasted_iota(jnp.int32, (8, 128), 1)
    tile_row = lax.broadcasted_iota(jnp.int32, (8, 128), 0)

    def surface(step, flag):
        def body(x, acc):
            at = jnp.where(turn_x, cx - 1 - x, x) * 4
            for yb in range(cy // 8):
                base = jnp.where(turn_y, cy // 8 - 1 - yb, yb) * (4 * cx) + at
                rows = slice(8 * yb, 8 * yb + 8)
                cols = (
                    -H[1, x + 1, rows, ZS : ZS + 1], H[0, x + 1, rows, ZS : ZS + 1],
                    E[1, x, rows, ZS : ZS + 1], -E[0, x, rows, ZS : ZS + 1],
                )
                for j in range(4):
                    acc = jnp.where(tile_lane == base + j, cols[j], acc)
            return acc

        tile = lax.fori_loop(0, cx, body, jnp.zeros((8, 128), F32)) * flag
        back = tile
        for bit in (1, 2, 4):
            back = jnp.where((tile_row & bit) != 0, pltpu.roll(back, bit, 0), pltpu.roll(back, 8 - bit, 0))
        G[step] = jnp.where(turn_y, back, tile)

    def peer(step, k):
        to = lax.rem(me + k, count)
        return pltpu.make_async_remote_copy(
            src_ref=G.at[step], dst_ref=g_out.at[step, me], send_sem=g1s.at[step, k], recv_sem=g1r.at[step, k],
            device_id=(to // ngy, lax.rem(to, ngy)), device_id_type=MESH)

    def own(step):
        return pltpu.make_async_copy(G.at[step], g_out.at[step, me], out_sem.at[3 + step])

    def gather_start(step):
        own(step).start()

        @pl.loop(1, count)
        def _(k):
            peer(step, k).start()

    def gather_end(step):
        own(step).wait()

        @pl.loop(1, count)
        def _(k):
            peer(step, k).wait()

    loads[0].wait()
    pl.semaphore_wait(barrier, ngx + ngy - 2)
    for k in range(1, ngy):
        pl.semaphore_signal(all_in, inc=1, device_id=(gx, lax.rem(gy + k, ngy)), device_id_type=MESH)
    blocks = range(cy // BY)
    send_y(0, 0)
    for block in blocks:
        send_x(0, 0, block)
    for load in loads[1:2] + loads[5:]:
        load.wait()

    coef = coefficients(nmat, nz, eps, delta, omega, damping)
    flag = flags[0, 0].astype(F32)

    for step in range(2):
        down, up = 2 * step, 2 * step + 1
        take_y(down, step)

        @pl.loop(0, cx - 1)
        def _(x):
            h_plane(step, x, blocks)

        for block in blocks:
            take_x(down, step, block)
            h_plane(step, cx - 1, [block])
            send_x(up, step, block)
        send_y(up, step)
        if step == 0:
            for load in loads[2:5]:
                load.wait()
        else:
            pltpu.make_async_copy(H.at[:, pl.ds(1, cx)], h_out, out_sem.at[0]).start()
            gather_start(0)
        sent_x(down, step)
        take_y(up, step)

        @pl.loop(1, cx)
        def _(x):
            e_plane(step, x, coef, blocks)

        for block in blocks:
            take_x(up, step, block)
            e_plane(step, 0, coef, [block])
            if step == 0:
                send_x(2, 1, block)
        if step == 0:
            send_y(2, 1)
            sent_x(up, step)
        surface(step, flag)
        if step == 0:
            pl.semaphore_wait(all_in, ngy - 1)
        else:
            gather_start(1)

    saves = [
        pltpu.make_async_copy(H.at[:, pl.ds(1, cx)], h_out, out_sem.at[0]),
        pltpu.make_async_copy(E.at[:, pl.ds(0, cx)], e_out, out_sem.at[1]),
        pltpu.make_async_copy(PA, p_out, out_sem.at[2]),
    ]
    saves[1].start()
    saves[2].start()
    sent_x(3, 1)
    for rnd in range(4):
        sent_y(rnd, rnd // 2)
    gather_end(0)
    gather_end(1)
    for save in saves:
        save.wait()


TILE = 1024
PART = 256
TABLES = 2 * 2 * 2


def angles():
    theta = (np.arange(NTH, dtype=np.float64)[:, None] + 0.5) * (math.pi / 2.0 / NTH)
    phi = (np.arange(NPH // 4, dtype=np.float64)[None, :] + 0.5) * (2.0 * math.pi / NPH)
    ux = (np.sin(theta) * np.cos(phi)).reshape(-1)
    uy = (np.sin(theta) * np.sin(phi)).reshape(-1)
    return ux, uy


def tiled(rows):
    return np.ascontiguousarray(rows.reshape(rows.shape[0], -1, TILE).swapaxes(0, 1))


def make_seeds(nx, ny):
    ux, uy = angles()
    x0, y0 = (nx - 1) / 2.0, (ny - 1) / 2.0
    rows = []
    for length in WAVELENGTHS:
        wave = 2.0 * math.pi / length
        for angle in (x0 * ux, (x0 - 1.0) * ux, -2.0 * ux, x0 * ux + y0 * uy, x0 * ux - y0 * uy):
            rows += [np.cos(wave * angle), np.sin(wave * angle)]
        rows += [np.zeros_like(ux)] * 6
    return tiled(np.stack(rows).astype(np.float32))


def make_tables(ny, cy):
    _, uy = angles()
    k = np.arange(ny // 2)
    group, lane = k // 128, k % 128
    y = (group * 4 + (lane % 32) // 8) * cy + (lane // 32) * 8 + lane % 8
    v = (ny - 1) / 2.0 - y
    rows = []
    for length in WAVELENGTHS:
        phase = (2.0 * math.pi / length) * v[:, None] * uy[None, :]
        for table in (np.cos(phase), np.sin(phase)):
            high = table.astype(np.float32).astype(BF16)
            rows += [high, (table - high.astype(np.float64)).astype(np.float32).astype(BF16)]
    return tiled(np.concatenate(rows))


def far_kernel(
    ngx, ngy, nx, ny, g_ref, seeds, tables, e_in, h_in, p_in, far, e_out, h_out, p_out,
    a_high, a_low, e_pass, h_pass, p_pass, sem,
):
    pid = pl.program_id(0)
    half = 2 * nx
    depth = ny // 2
    fields = enumerate(zip((e_in, h_in, p_in), (e_pass, h_pass, p_pass), (e_out, h_out, p_out)))
    moves = [
        (pltpu.make_async_copy(src, mid, sem.at[0, i]), pltpu.make_async_copy(mid, dst, sem.at[1, i]))
        for i, (src, mid, dst) in fields
    ]

    @pl.when(pid == 0)
    def _():
        for load, _ in moves:
            load.start()
        quarter = lax.broadcasted_iota(jnp.int32, (32, 128), 1) // 32
        for s in range(2):
            for x in range(ngx // 2):
                for group in range(ngy // 8):
                    kinds = [[], [], [], []]
                    for y in range(4 * group, 4 * group + 4):
                        low_x, high_x = x * ngy, (ngx - 1 - x) * ngy
                        t00, t10 = g_ref[s, low_x + y], g_ref[s, high_x + y]
                        t01, t11 = g_ref[s, low_x + ngy - 1 - y], g_ref[s, high_x + ngy - 1 - y]
                        even0, even1, odd0, odd1 = t10 + t00, t11 + t01, t10 - t00, t11 - t01
                        for kind, tile in zip(kinds, (even0 + even1, odd0 + odd1, even1 - even0, odd1 - odd0)):
                            kind.append(tile)
                    turned = jnp.concatenate(kinds[0] + kinds[1] + kinds[2] + kinds[3], axis=0).T
                    for kind in range(4):
                        block = jnp.zeros((32, 128), F32)
                        for yb in range(4):
                            piece = turned[32 * yb : 32 * yb + 32, :]
                            shift = (32 * (yb - kind)) % 128
                            if shift:
                                piece = pltpu.roll(piece, shift, 1)
                            block = jnp.where(quarter == yb, piece, block)
                        high = block.astype(BF16)
                        rows = pl.ds((2 * s + kind % 2) * half + 32 * x, 32)
                        lanes = pl.ds(128 * group, 128)
                        a_high[kind // 2, rows, lanes] = high
                        a_low[kind // 2, rows, lanes] = (block - high.astype(F32)).astype(BF16)

    @pl.when(pid == 1)
    def _():
        for load, save in moves:
            load.wait()
            save.start()

    scale = 1.0 / math.sqrt(nx * ny)
    sub = lax.broadcasted_iota(jnp.int32, (8, PART), 0)
    top = sub < 4
    lane = lax.broadcasted_iota(jnp.int32, (8, 128), 1)
    first = lane < 64
    mirror = 127 - lane

    def times(a, b):
        return (a[0] * b[0] - a[1] * b[1], a[0] * b[1] + a[1] * b[0])

    for o in range(0, TILE, PART):
        lanes = slice(o, o + PART)
        for f in range(2):
            omega = 2.0 * math.pi / WAVELENGTHS[f]
            kappa = [math.cos(omega * (s + 1) * DT) * scale for s in range(2)]
            sigma = [math.sin(omega * (s + 1) * DT) * scale for s in range(2)]

            def seed(i):
                row = 16 * f + i
                return jnp.broadcast_to(seeds[0, row : row + 1, lanes], (8, PART))

            sums = []
            for trig in range(2):
                at = (2 * f + trig) * 2 * depth
                high = tables[0, at : at + depth, lanes]
                low = tables[0, at + depth : at + 2 * depth, lanes]
                ah, al = a_high[trig], a_low[trig]
                sums.append(jnp.dot(
                    jnp.concatenate([ah, ah, al], axis=1), jnp.concatenate([high, low, high], axis=0),
                    preferred_element_type=F32))
            w = (jnp.where(top, seed(0), seed(2)), jnp.where(top, seed(1), seed(3)))
            e2 = (seed(4), seed(5))
            acc = [[None] * 4, [None] * 4]
            for g in range(nx // 4):
                for s in range(2):
                    for trig in range(2):
                        for odd in range(2):
                            at = (2 * s + odd) * half + 8 * g
                            term = sums[trig][at : at + 8, :] * w[odd]
                            i = 2 * trig + odd
                            acc[s][i] = term if g == 0 else acc[s][i] + term
                if g + 1 < nx // 4:
                    w = times(w, e2)
            ck, sk, dk, rk = [acc[0][i] * kappa[0] + acc[1][i] * kappa[1] for i in range(4)]
            cg, sg, dg, rg = [acc[0][i] * sigma[0] + acc[1][i] * sigma[1] for i in range(4)]
            re_same, re_diff = ck - rk, ck + rk
            im_same, im_diff = cg - rg, cg + rg
            plus_k, minus_k = sk + dk, sk - dk
            plus_g, minus_g = sg + dg, sg - dg
            quads = (
                (re_same + plus_g, plus_k - im_same),
                (re_diff - minus_g, -minus_k - im_diff),
                (re_same - plus_g, -plus_k - im_same),
                (re_diff + minus_g, minus_k - im_diff),
            )
            same = (seed(6), jnp.where(top, -seed(7), seed(7)))
            diff = (seed(8), jnp.where(top, -seed(9), seed(9)))
            done = []
            for q, (re, im) in enumerate(quads):
                both = jnp.where(top, re, im) + pltpu.roll(jnp.where(top, im, re), 4, 0)
                turn = (same, diff)[q % 2]
                swing = pltpu.roll(both, 4, 0) * turn[1]
                done.append(both * turn[0] + (swing if q in (0, 3) else -swing))
            for pair in range(PART // 128):
                cut = slice(128 * pair, 128 * pair + 128)
                for h in range(2):
                    here, back = done[2 * h][:, cut], jnp.take_along_axis(done[2 * h + 1][:, cut], mirror, axis=1)
                    both = (jnp.where(first, here, back), pltpu.roll(jnp.where(first, back, here), 64, 1))
                    for t in range(2):
                        d = (2 * (o // 128 + pair) + t) * 256 + h * 128
                        far[f, 0, :, d : d + 128] = both[t][0:4]
                        far[f, 1, :, d : d + 128] = both[t][4:8]

    @pl.when(pid == pl.num_programs(0) - 1)
    def _():
        for _, save in moves:
            save.wait()


def shards(
    e_field, h_field, polar, polar_prev, material,
    eps_table, delta_table, omega_table, damping_table, surface_flags,
):
    _, cx, cy, nz = e_field.shape
    ngx, ngy = lax.axis_size("gx"), lax.axis_size("gy")
    nx, ny = ngx * cx, ngy * cy
    width = 4 * nx
    hbm = pl.BlockSpec(memory_space=pl.ANY)
    field = jax.ShapeDtypeStruct(e_field.shape, F32)
    dma = pltpu.SemaphoreType.DMA
    e, h, p, g = pl.pallas_call(
        functools.partial(step_kernel, ngx, ngy, eps_table.shape[0]),
        out_shape=(field, field, field, jax.ShapeDtypeStruct((2, ngx * ngy, 8, 128), F32)),
        in_specs=[hbm] * 10,
        out_specs=(hbm,) * 4,
        scratch_shapes=[
            pltpu.VMEM((3, cx + 1, cy, nz), F32),
            pltpu.VMEM((3, cx + 1, cy, nz), F32),
            pltpu.VMEM((3, cx, cy, nz), F32),
            pltpu.VMEM((3, cx, cy, nz), F32),
            pltpu.VMEM((cx, cy, nz), jnp.int32),
            pltpu.VMEM((4, 2, cx, nz), F32),
            pltpu.VMEM((2, 2, cx, nz), F32),
            pltpu.VMEM((2, 2, cx, nz), F32),
            pltpu.VMEM((2, 8, 128), F32),
            *[pltpu.SMEM(table.shape, F32) for table in (eps_table, delta_table, omega_table, damping_table)],
            pltpu.SMEM(surface_flags.shape, jnp.int32),
            dma((10,)), dma((5,)), dma((4, 2 * (cy // BY))), dma((4, 2 * (cy // BY))), dma((4,)), dma((4,)),
            dma((2, ngx * ngy)), dma((2, ngx * ngy)), pltpu.SemaphoreType.REGULAR,
        ],
        compiler_params=pltpu.CompilerParams(
            collective_id=0, has_side_effects=True, vmem_limit_bytes=58 * 1024 * 1024),
    )(e_field, h_field, polar, polar_prev, material,
      eps_table, delta_table, omega_table, damping_table, surface_flags)

    steps = (NDIR // 4) // TILE
    seeds, tables = make_seeds(nx, ny), make_tables(ny, cy)
    far, e, h, p = pl.pallas_call(
        functools.partial(far_kernel, ngx, ngy, nx, ny),
        grid=(steps,),
        out_shape=(jax.ShapeDtypeStruct((2, 2, 4, NDIR), F32), field, field, field),
        in_specs=[
            pl.BlockSpec(g.shape, lambda i: (0, 0, 0, 0)),
            pl.BlockSpec((1, *seeds.shape[1:]), lambda i: (i, 0, 0)),
            pl.BlockSpec((1, *tables.shape[1:]), lambda i: (i, 0, 0)),
            hbm, hbm, hbm,
        ],
        out_specs=(pl.BlockSpec((2, 2, 4, 4 * TILE), lambda i: (0, 0, 0, i)), hbm, hbm, hbm),
        scratch_shapes=[
            pltpu.VMEM((2, 2 * width, ny // 2), BF16),
            pltpu.VMEM((2, 2 * width, ny // 2), BF16),
            *[pltpu.VMEM(e_field.shape, F32)] * 3,
            dma((2, 3)),
        ],
        compiler_params=pltpu.CompilerParams(vmem_limit_bytes=56 * 1024 * 1024),
    )(g, jnp.asarray(seeds), jnp.asarray(tables), e, h, p)
    return e, h, p, far


def solution(mesh):
    cells = P(None, "gx", "gy", None)
    placed = (cells, cells, cells, cells, P("gx", "gy", None), P(), P(), P(), P(), P("gx", "gy"))
    return jax.shard_map(
        shards, mesh=mesh, in_specs=placed, out_specs=(cells, cells, cells, P()), check_vma=False,
    )
```

time: 48.5 us -> 42.3 us (0.87)
  Pallas kernels: 44.7 us -> 40.8 us
  local copies, waits for them, and re-layouts: 2.26 us -> 0 us
    pallas_call x2 -> x1, Pallas kernels: 13.2 us -> 10.2 us  [shards(): pl.pallas_call(functools.partial(far_kernel, ngx, ngy, nx, ny), grid=(ste...]
    unnamed x1 -> x0, local copies, waits for them, and re-layouts: 2.26 us -> none
    pallas_call x1, Pallas kernels: 31.5 us -> 30.7 us  [shards(): pl.pallas_call(functools.partial(step_kernel, ngx, ngy, eps_table.shape[0...]
where the time goes in v1:
time: 42.3 us; the launch traced here: 42.1 us
  Pallas kernels  40.8 us (96%)
  between operations  1.29 us (3%)
    pallas_call x1, Pallas kernels, shards(): pl.pallas_call(functools.partial(step_kernel, ngx, ngy, eps_table.shape[0...  30.7 us
    pallas_call x1, Pallas kernels, shards(): pl.pallas_call(functools.partial(far_kernel, ngx, ngy, nx, ny), grid=(ste...  10.2 us

profile of v1, /device:TPU:0, one launch (start us, length us, event | category | flops | bytes accessed | tf_op | source)
XLA Modules:
  0.0 42.1 jit_solution(15393499174261079671)
XLA Ops:
  1.3 30.7 %shard_map.147 = (f32[3,8,32,512]{3,2,1,0:T(8,128)}, f32[3,8,32,512]{3,2,1,0:T(8,128)}, f32[3,8,32,512]{3,2,1,0:T(8,128)}, f32[2,32,8,128]{3,2,1,0:T(8,128)}) custom-call(f32[3,8,32,512]{3,2,1,0:T(8,128)} %e_in.1, f32[3,8,32,512]{3,2,1,0:T(8,128)} %h_in.1, f32[3,8,32,512]{3,2,1,0:T(8,128)} %p_in.1, f32[3,8,32,512]{3,2,1,0:T(8,128)} %q_in.1, ...), custom_call_target="tpu_custom_call" | custom-call | tf_op jit(solution)/shard_map/pallas_call | solution.py:516
  32.0 10.2 %shard_map.148 = (f32[2,2,4,16384]{3,2,1,0:T(4,128)}, f32[3,8,32,512]{3,2,1,0:T(8,128)}, f32[3,8,32,512]{3,2,1,0:T(8,128)}, f32[3,8,32,512]{3,2,1,0:T(8,128)}) custom-call(f32[2,32,8,128]{3,2,1,0:T(8,128)} %get-tuple-element.12.g_ref, f32[4,32,1024]{2,1,0:T(8,128)} %constant.4.clone.seeds, bf16[4,1024,1024]{2,1,0:T(8,128)(2,1)} %constant.5.clone.tables, ...), custom_call_target="tpu_custom_call" | custom-call | tf_op jit(solution)/shard_map/pallas_call | solution.py:543

commit v2 on v1

--- a/solution.py
+++ b/solution.py
@@ -41,16 +41,16 @@
     ngx, ngy, nmat,
     e_in, h_in, p_in, q_in, m_in, eps_in, delta_in, omega_in, damping_in, flags_in,
     e_out, h_out, p_out, g_out,
-    E, H, PA, PB, MAT, ystage, ye, yh, G, eps, delta, omega, damping, flags,
-    in_sem, out_sem, xs_sem, xr_sem, ys_sem, yr_sem, g1s, g1r, all_in,
+    E, H, PA, PB, MAT, xstage, ystage, cstage, xe, xh, ye, yh, ce, G, eps, delta, omega, damping, flags,
+    in_sem, out_sem, xs_sem, xr_sem, ys_sem, yr_sem, cs_sem, cr_sem, g1s, g1r, all_in,
 ):
     cx, cy, nz = MAT.shape
     gx = lax.axis_index("gx")
     gy = lax.axis_index("gy")
 
     loads = [
-        pltpu.make_async_copy(e_in, E.at[:, pl.ds(0, cx)], in_sem.at[0]),
-        pltpu.make_async_copy(h_in, H.at[:, pl.ds(1, cx)], in_sem.at[1]),
+        pltpu.make_async_copy(e_in, E, in_sem.at[0]),
+        pltpu.make_async_copy(h_in, H, in_sem.at[1]),
         pltpu.make_async_copy(p_in, PA, in_sem.at[2]),
         pltpu.make_async_copy(q_in, PB, in_sem.at[3]),
         pltpu.make_async_copy(m_in, MAT, in_sem.at[4]),
@@ -69,103 +69,143 @@
     for k in range(1, ngy):
         pl.semaphore_signal(barrier, inc=1, device_id=(gx, lax.rem(gy + k, ngy)), device_id_type=MESH)
 
-    @pl.when(gx == ngx - 1)
-    def _():
-        for c in (1, 2):
-            E[c, cx] = jnp.zeros((cy, nz), F32)
-
-    @pl.when(gx == 0)
-    def _():
-        for c in (1, 2):
-            H[c, 0] = jnp.zeros((cy, nz), F32)
-
-    @pl.when(gy == ngy - 1)
-    def _():
-        ye[...] = jnp.zeros(ye.shape, F32)
-
-    @pl.when(gy == 0)
-    def _():
-        yh[...] = jnp.zeros(yh.shape, F32)
-
-    def copies(rnd, step):
-        if rnd % 2 == 0:
-            field, at_src, at_dst, ydst = E, 0, cx, ye.at[step]
-            tx, ty = gx - 1, gy - 1
-            sends_x, sends_y = gx > 0, gy > 0
-            takes_x, takes_y = gx < ngx - 1, gy < ngy - 1
+    for dx, dy in ((1, ngy - 1), (ngx - 1, 1)):
+        pl.semaphore_signal(
+            barrier, inc=1, device_id=(lax.rem(gx + dx, ngx), lax.rem(gy + dy, ngy)), device_id_type=MESH)
+
+    not_low_x, not_high_x = gx > 0, gx < ngx - 1
+    not_low_y, not_high_y = gy > 0, gy < ngy - 1
+    dt_x = jnp.where(not_low_x, DT, 0.0)
+    dt_y = jnp.where(not_low_y, DT, 0.0)
+
+    def clear(ref):
+        ref[...] = jnp.zeros(ref.shape, F32)
+
+    pl.when(gx == ngx - 1)(lambda: clear(xe))
+    pl.when(gx == 0)(lambda: clear(xh))
+    pl.when(gy == ngy - 1)(lambda: clear(ye))
+    pl.when(gy == 0)(lambda: clear(yh))
+    for kind, there in ((0, not_low_x & not_high_y), (1, not_high_x & not_low_y)):
+
+        @pl.when(jnp.logical_not(there))
+        def _():
+            for step in range(2):
+                ce[step, kind] = jnp.zeros((1, nz), F32)
+
+    sends_x, takes_x = (not_low_x, not_high_x), (not_high_x, not_low_x)
+    sends_y, takes_y = (not_low_y, not_high_y), (not_high_y, not_low_y)
+
+    def x_copies(step, way, block):
+        copies = []
+        for i in range(2):
+            rows = pl.ds(block * BY, BY)
+            src = E.at[1 + i, 0, rows] if way == 0 else xstage.at[step, i, rows]
+            dst = (xe, xh)[way].at[step, i, rows]
+            sem = 2 * block + i
+            copies.append(pltpu.make_async_remote_copy(
+                src_ref=src, dst_ref=dst, send_sem=xs_sem.at[step, way, sem], recv_sem=xr_sem.at[step, way, sem],
+                device_id=(lax.rem(gx + (ngx - 1, 1)[way], ngx), gy), device_id_type=MESH))
+        return copies
+
+    def y_copy(step, way):
+        return pltpu.make_async_remote_copy(
+            src_ref=ystage.at[step, way], dst_ref=(ye, yh)[way].at[step],
+            send_sem=ys_sem.at[step, way], recv_sem=yr_sem.at[step, way],
+            device_id=(gx, lax.rem(gy + (ngy - 1, 1)[way], ngy)), device_id_type=MESH)
+
+    sends_c = (not_high_x & not_low_y, not_low_x & not_high_y)
+    takes_c = (not_low_x & not_high_y, not_high_x & not_low_y)
+
+    def c_copy(step, kind):
+        dx, dy = ((1, ngy - 1), (ngx - 1, 1))[kind]
+        return pltpu.make_async_remote_copy(
+            src_ref=cstage.at[step, kind], dst_ref=ce.at[step, kind],
+            send_sem=cs_sem.at[step, kind], recv_sem=cr_sem.at[step, kind],
+            device_id=(lax.rem(gx + dx, ngx), lax.rem(gy + dy, ngy)), device_id_type=MESH)
+
+    def send_x(step, way, block):
+        @pl.when(sends_x[way])
+        def _():
+            for copy in x_copies(step, way, block):
+                copy.start()
+
+    def take_x(step, way, block):
+        @pl.when(takes_x[way])
+        def _():
+            for copy in x_copies(step, way, block):
+                copy.wait_recv()
+
+    def sent_x(step, way):
+        @pl.when(sends_x[way])
+        def _():
+            for block in blocks:
+                for copy in x_copies(step, way, block):
+                    copy.wait_send()
+
+    def send_y(step, way):
+        pl.when(sends_y[way])(lambda: y_copy(step, way).start())
+
+    def take_y(step, way):
+        pl.when(takes_y[way])(lambda: y_copy(step, way).wait_recv())
+
+    def sent_y(step, way):
+        pl.when(sends_y[way])(lambda: y_copy(step, way).wait_send())
+
+    def send_c(step, kind):
+        if kind == 0:
+            cstage[step, 0] = E[0, cx - 1, 0:1, :]
         else:
-            field, at_src, at_dst, ydst = H, cx, 0, yh.at[step]
-            tx, ty = gx + 1, gy + 1
-            sends_x, sends_y = gx < ngx - 1, gy < ngy - 1
-            takes_x, takes_y = gx > 0, gy > 0
-        xcopies = []
-        for i in range(2 * (cy // BY)):
-            c, y = 1 + i % 2, (i // 2) * BY
-            xcopies.append(pltpu.make_async_remote_copy(
-                src_ref=field.at[c, at_src, pl.ds(y, BY)], dst_ref=field.at[c, at_dst, pl.ds(y, BY)],
-                send_sem=xs_sem.at[rnd, i], recv_sem=xr_sem.at[rnd, i],
-                device_id=(lax.rem(tx + ngx, ngx), gy), device_id_type=MESH))
-        ycopy = pltpu.make_async_remote_copy(
-            src_ref=ystage.at[rnd], dst_ref=ydst, send_sem=ys_sem.at[rnd], recv_sem=yr_sem.at[rnd],
-            device_id=(gx, lax.rem(ty + ngy, ngy)), device_id_type=MESH)
-        return xcopies, ycopy, sends_x, sends_y, takes_x, takes_y
-
-    def send_x(rnd, step, block):
-        xcopies, _, sends_x, _, _, _ = copies(rnd, step)
-
-        @pl.when(sends_x)
-        def _():
-            for xcopy in xcopies[2 * block : 2 * block + 2]:
-                xcopy.start()
-
-    def send_y(rnd, step):
-        _, ycopy, _, sends_y, _, _ = copies(rnd, step)
+            cstage[step, 1] = E[1, 0, cy - 1 : cy, :]
+        pl.when(sends_c[kind])(lambda: c_copy(step, kind).start())
+
+    def take_c(step, kind):
+        pl.when(takes_c[kind])(lambda: c_copy(step, kind).wait_recv())
+
+    def sent_c(step, kind):
+        pl.when(sends_c[kind])(lambda: c_copy(step, kind).wait_send())
+
+    blocks = range(cy // BY)
+    last = cy // BY - 1
+
+    row_id = lax.broadcasted_iota(jnp.int32, (BY, nz), 0)
+    lane_id = lax.broadcasted_iota(jnp.int32, (BY, nz), 1)
+
+    def up_y(v, row):
+        return jnp.where(row_id == BY - 1, row, pltpu.roll(v, BY - 1, 0))
+
+    def up_z(v):
+        return jnp.where(lane_id == nz - 1, 0.0, pltpu.roll(v, nz - 1, 1))
+
+    def down_y(v, row):
+        return jnp.where(row_id == 0, row, pltpu.roll(v, 1, 0))
+
+    def down_z(v):
+        return jnp.where(lane_id == 0, 0.0, pltpu.roll(v, 1, 1))
+
+    def part_x(step, block):
+        here, x, y = pl.ds(block * BY, BY), cx - 1, block * BY
+        ex, ey, ez = E[0, x, here, :], E[1, x, here, :], E[2, x, here, :]
+        rx = E[0, x, y + BY : y + BY + 1, :] if block < last else jnp.zeros((1, nz), F32)
+        xstage[step, 0, here, :] = H[1, x, here, :] - DT * ((up_z(ex) - ex) + ez)
+        xstage[step, 1, here, :] = H[2, x, here, :] + DT * (ey + (up_y(ex, rx) - ex))
+        send_x(step, 1, block)
+
+    def part_y(step):
+        here = pl.ds(cy - BY, BY)
+        for x in range(cx):
+            ex, ey, ez = E[0, x, here, :], E[1, x, here, :], E[2, x, here, :]
+            slope = E[1, x + 1, here, :] - ey if x < cx - 1 else -ey
+            part_hx = H[0, x, here, :] + DT * (ez + (up_z(ey) - ey))
+            part_hz = H[2, x, here, :] - DT * (slope + ex)
+            ystage[step, 1, 0, x : x + 1, :] = part_hx[BY - 1 : BY, :]
+            ystage[step, 1, 1, x : x + 1, :] = part_hz[BY - 1 : BY, :]
+        send_y(step, 1)
+
+    def rows_y(step):
         for i, c in enumerate((0, 2)):
             for x in range(cx):
-                if rnd % 2 == 0:
-                    ystage[rnd, i, x : x + 1, :] = E[c, x, 0:1, :]
-                else:
-                    ystage[rnd, i, x : x + 1, :] = H[c, x + 1, cy - 1 : cy, :]
-        pl.when(sends_y)(ycopy.start)
-
-    def take_x(rnd, step, block):
-        xcopies, _, _, _, takes_x, _ = copies(rnd, step)
-
-        @pl.when(takes_x)
-        def _():
-            for xcopy in xcopies[2 * block : 2 * block + 2]:
-                xcopy.wait_recv()
-
-    def take_y(rnd, step):
-        _, ycopy, _, _, _, takes_y = copies(rnd, step)
-        pl.when(takes_y)(ycopy.wait_recv)
-
-    def sent_x(rnd, step):
-        xcopies, _, sends_x, _, _, _ = copies(rnd, step)
-
-        @pl.when(sends_x)
-        def _():
-            for xcopy in xcopies:
-                xcopy.wait_send()
-
-    def sent_y(rnd, step):
-        _, ycopy, _, sends_y, _, _ = copies(rnd, step)
-        pl.when(sends_y)(ycopy.wait_send)
-
-    row_id = lax.broadcasted_iota(jnp.int32, (BY, nz), 0)
-    lane_id = lax.broadcasted_iota(jnp.int32, (BY, nz), 1)
-
-    def up_y(v, row):
-        return jnp.where(row_id == BY - 1, row, pltpu.roll(v, BY - 1, 0))
-
-    def up_z(v):
-        return jnp.where(lane_id == nz - 1, 0.0, pltpu.roll(v, nz - 1, 1))
-
-    def down_y(v, row):
-        return jnp.where(row_id == 0, row, pltpu.roll(v, 1, 0))
-
-    def down_z(v):
-        return jnp.where(lane_id == 0, 0.0, pltpu.roll(v, 1, 1))
+                ystage[step, 0, i, x : x + 1, :] = E[c, x, 0:1, :]
+        send_y(step, 0)
 
     def h_plane(step, x, blocks):
         for y in [BY * block for block in blocks]:
@@ -175,16 +215,20 @@
                 rx, rz = E[0, x, y + BY : y + BY + 1, :], E[2, x, y + BY : y + BY + 1, :]
             else:
                 rx, rz = ye[step, 0, pl.ds(x, 1), :], ye[step, 1, pl.ds(x, 1), :]
-            eyx, ezx = E[1, x + 1, here, :], E[2, x + 1, here, :]
+            if isinstance(x, int) and x == cx - 1:
+                eyx, ezx = xe[step, 0, here, :], xe[step, 1, here, :]
+            else:
+                eyx, ezx = E[1, x + 1, here, :], E[2, x + 1, here, :]
             curl_x = (up_y(ez, rz) - ez) - (up_z(ey) - ey)
             curl_y = (up_z(ex) - ex) - (ezx - ez)
             curl_z = (eyx - ey) - (up_y(ex, rx) - ex)
-            H[0, x + 1, here, :] = H[0, x + 1, here, :] - DT * curl_x
-            H[1, x + 1, here, :] = H[1, x + 1, here, :] - DT * curl_y
-            H[2, x + 1, here, :] = H[2, x + 1, here, :] - DT * curl_z
+            H[0, x, here, :] = H[0, x, here, :] - DT * curl_x
+            H[1, x, here, :] = H[1, x, here, :] - DT * curl_y
+            H[2, x, here, :] = H[2, x, here, :] - DT * curl_z
 
     def e_plane(step, x, coef, blocks):
         now, old = (PA, PB) if step == 0 else (PB, PA)
+        fixed = isinstance(x, int)
         for y in [BY * block for block in blocks]:
             here = pl.ds(y, BY)
             mat = MAT[x, here, :]
@@ -193,12 +237,23 @@
                 hit = mat == m
                 vox = [jnp.where(hit, coef[m][i], vox[i]) for i in range(4)]
             a, b, c, inv = vox
-            hx, hy, hz = H[0, x + 1, here, :], H[1, x + 1, here, :], H[2, x + 1, here, :]
+            hx, hy, hz = H[0, x, here, :], H[1, x, here, :], H[2, x, here, :]
             if y > 0:
-                rx, rz = H[0, x + 1, y - 1 : y, :], H[2, x + 1, y - 1 : y, :]
+                rx, rz = H[0, x, y - 1 : y, :], H[2, x, y - 1 : y, :]
             else:
-                rx, rz = yh[step, 0, pl.ds(x, 1), :], yh[step, 1, pl.ds(x, 1), :]
-            hyx, hzx = H[1, x, here, :], H[2, x, here, :]
+                rx = yh[step, 0, pl.ds(x, 1), :] - dt_y * E[2, x, 0:1, :]
+                edge = E[0, x, 0:1, :]
+                if fixed and x == cx - 1:
+                    edge = edge - ce[step, 1]
+                rz = yh[step, 1, pl.ds(x, 1), :] + dt_y * edge
+            if fixed and x == 0:
+                hyx = xh[step, 0, here, :] + dt_x * E[2, 0, here, :]
+                edge = E[1, 0, here, :]
+                if y + BY == cy:
+                    edge = jnp.where(row_id == BY - 1, edge - ce[step, 0], edge)
+                hzx = xh[step, 1, here, :] - dt_x * edge
+            else:
+                hyx, hzx = H[1, x - 1, here, :], H[2, x - 1, here, :]
             curls = (
                 (hz - down_y(hz, rz)) - (hy - down_z(hy)),
                 (hx - down_z(hx)) - (hz - hzx),
@@ -223,7 +278,7 @@
                 base = jnp.where(turn_y, cy // 8 - 1 - yb, yb) * (4 * cx) + at
                 rows = slice(8 * yb, 8 * yb + 8)
                 cols = (
-                    -H[1, x + 1, rows, ZS : ZS + 1], H[0, x + 1, rows, ZS : ZS + 1],
+                    -H[1, x, rows, ZS : ZS + 1], H[0, x, rows, ZS : ZS + 1],
                     E[1, x, rows, ZS : ZS + 1], -E[0, x, rows, ZS : ZS + 1],
                 )
                 for j in range(4):
@@ -260,53 +315,79 @@
             peer(step, k).wait()
 
     loads[0].wait()
-    pl.semaphore_wait(barrier, ngx + ngy - 2)
+    pl.semaphore_wait(barrier, ngx + ngy)
+    send_c(0, 0)
+    send_c(0, 1)
+    for block in blocks:
+        send_x(0, 0, block)
+    rows_y(0)
+    loads[1].wait()
+    for block in blocks:
+        part_x(0, block)
+    part_y(0)
     for k in range(1, ngy):
         pl.semaphore_signal(all_in, inc=1, device_id=(gx, lax.rem(gy + k, ngy)), device_id_type=MESH)
-    blocks = range(cy // BY)
-    send_y(0, 0)
-    for block in blocks:
-        send_x(0, 0, block)
-    for load in loads[1:2] + loads[5:]:
+    for load in loads[5:]:
         load.wait()
 
     coef = coefficients(nmat, nz, eps, delta, omega, damping)
     flag = flags[0, 0].astype(F32)
 
     for step in range(2):
-        down, up = 2 * step, 2 * step + 1
-        take_y(down, step)
 
         @pl.loop(0, cx - 1)
         def _(x):
-            h_plane(step, x, blocks)
-
-        for block in blocks:
-            take_x(down, step, block)
-            h_plane(step, cx - 1, [block])
-            send_x(up, step, block)
-        send_y(up, step)
+            h_plane(step, x, range(last))
+
         if step == 0:
             for load in loads[2:5]:
                 load.wait()
         else:
-            pltpu.make_async_copy(H.at[:, pl.ds(1, cx)], h_out, out_sem.at[0]).start()
             gather_start(0)
-        sent_x(down, step)
-        take_y(up, step)
-
-        @pl.loop(1, cx)
+
+        @pl.loop(1, cx - 1)
         def _(x):
-            e_plane(step, x, coef, blocks)
-
+            e_plane(step, x, coef, range(1, last))
+
+        for block in range(last):
+            take_x(step, 0, block)
+            h_plane(step, cx - 1, [block])
+        take_y(step, 0)
+        take_x(step, 0, last)
+        h_plane(step, cx - 1, [last])
+
+        @pl.loop(0, cx - 1)
+        def _(x):
+            h_plane(step, x, [last])
+
+        if step == 1:
+            pltpu.make_async_copy(H, h_out, out_sem.at[0]).start()
+        sent_x(step, 0)
+        take_y(step, 1)
+        take_c(step, 1)
+        for block in range(last, -1, -1):
+            e_plane(step, cx - 1, coef, [block])
+            if step == 0:
+                part_x(1, block)
+        if step == 0:
+            send_c(1, 0)
         for block in blocks:
-            take_x(up, step, block)
+            take_x(step, 1, block)
+            if block == last:
+                take_c(step, 0)
             e_plane(step, 0, coef, [block])
             if step == 0:
-                send_x(2, 1, block)
+                send_x(1, 0, block)
         if step == 0:
-            send_y(2, 1)
-            sent_x(up, step)
+            send_c(1, 1)
+
+        @pl.loop(1, cx - 1)
+        def _(x):
+            e_plane(step, x, coef, [0, last])
+
+        if step == 0:
+            rows_y(1)
+            part_y(1)
         surface(step, flag)
         if step == 0:
             pl.semaphore_wait(all_in, ngy - 1)
@@ -314,15 +395,17 @@
             gather_start(1)
 
     saves = [
-        pltpu.make_async_copy(H.at[:, pl.ds(1, cx)], h_out, out_sem.at[0]),
-        pltpu.make_async_copy(E.at[:, pl.ds(0, cx)], e_out, out_sem.at[1]),
+        pltpu.make_async_copy(H, h_out, out_sem.at[0]),
+        pltpu.make_async_copy(E, e_out, out_sem.at[1]),
         pltpu.make_async_copy(PA, p_out, out_sem.at[2]),
     ]
     saves[1].start()
     saves[2].start()
-    sent_x(3, 1)
-    for rnd in range(4):
-        sent_y(rnd, rnd // 2)
+    for step in range(2):
+        sent_x(step, 1)
+        for i in range(2):
+            sent_y(step, i)
+            sent_c(step, i)
     gather_end(0)
     gather_end(1)
     for save in saves:
@@ -331,7 +414,6 @@
 
 TILE = 1024
 PART = 256
-TABLES = 2 * 2 * 2
 
 
 def angles():
@@ -352,34 +434,22 @@
     rows = []
     for length in WAVELENGTHS:
         wave = 2.0 * math.pi / length
-        for angle in (x0 * ux, (x0 - 1.0) * ux, -2.0 * ux, x0 * ux + y0 * uy, x0 * ux - y0 * uy):
+        turns = [(y0 - y) * uy for y in range(8)]
+        rows += [np.cos(wave * angle) for angle in turns] + [np.sin(wave * angle) for angle in turns]
+        for angle in (x0 * ux, (x0 - 1.0) * ux, -2.0 * ux, x0 * ux + y0 * uy, x0 * ux - y0 * uy, -8.0 * uy, -16.0 * uy):
             rows += [np.cos(wave * angle), np.sin(wave * angle)]
-        rows += [np.zeros_like(ux)] * 6
+        rows += [np.zeros_like(ux)] * 2
     return tiled(np.stack(rows).astype(np.float32))
 
 
-def make_tables(ny, cy):
-    _, uy = angles()
-    k = np.arange(ny // 2)
-    group, lane = k // 128, k % 128
-    y = (group * 4 + (lane % 32) // 8) * cy + (lane // 32) * 8 + lane % 8
-    v = (ny - 1) / 2.0 - y
-    rows = []
-    for length in WAVELENGTHS:
-        phase = (2.0 * math.pi / length) * v[:, None] * uy[None, :]
-        for table in (np.cos(phase), np.sin(phase)):
-            high = table.astype(np.float32).astype(BF16)
-            rows += [high, (table - high.astype(np.float64)).astype(np.float32).astype(BF16)]
-    return tiled(np.concatenate(rows))
-
-
 def far_kernel(
-    ngx, ngy, nx, ny, g_ref, seeds, tables, e_in, h_in, p_in, far, e_out, h_out, p_out,
+    ngx, ngy, nx, ny, g_ref, seeds, e_in, h_in, p_in, far, e_out, h_out, p_out,
     a_high, a_low, e_pass, h_pass, p_pass, sem,
 ):
     pid = pl.program_id(0)
     half = 2 * nx
     depth = ny // 2
+    per = ny // ngy // 8
     fields = enumerate(zip((e_in, h_in, p_in), (e_pass, h_pass, p_pass), (e_out, h_out, p_out)))
     moves = [
         (pltpu.make_async_copy(src, mid, sem.at[0, i]), pltpu.make_async_copy(mid, dst, sem.at[1, i]))
@@ -441,14 +511,25 @@
             sigma = [math.sin(omega * (s + 1) * DT) * scale for s in range(2)]
 
             def seed(i):
-                row = 16 * f + i
+                row = 32 * f + 16 + i
                 return jnp.broadcast_to(seeds[0, row : row + 1, lanes], (8, PART))
 
+            v = (seeds[0, 32 * f : 32 * f + 8, lanes], seeds[0, 32 * f + 8 : 32 * f + 16, lanes])
+            e16 = (seed(12), seed(13))
+            w = times(v, (seed(10), seed(11)))
+            waves = []
+            for j in range(depth // 16):
+                waves += [v, w]
+                if 16 * (j + 1) < depth:
+                    v, w = times(v, e16), times(w, e16)
+            order = [
+                (4 * group + y) * per + yb for group in range(depth // 128) for yb in range(per) for y in range(4)
+            ]
             sums = []
             for trig in range(2):
-                at = (2 * f + trig) * 2 * depth
-                high = tables[0, at : at + depth, lanes]
-                low = tables[0, at + depth : at + 2 * depth, lanes]
+                full = jnp.concatenate([waves[j][trig] for j in order], axis=0)
+                high = full.astype(BF16)
+                low = (full - high.astype(F32)).astype(BF16)
                 ah, al = a_high[trig], a_low[trig]
                 sums.append(jnp.dot(
                     jnp.concatenate([ah, ah, al], axis=1), jnp.concatenate([high, low, high], axis=0),
@@ -519,18 +600,20 @@
         in_specs=[hbm] * 10,
         out_specs=(hbm,) * 4,
         scratch_shapes=[
-            pltpu.VMEM((3, cx + 1, cy, nz), F32),
-            pltpu.VMEM((3, cx + 1, cy, nz), F32),
-            pltpu.VMEM((3, cx, cy, nz), F32),
-            pltpu.VMEM((3, cx, cy, nz), F32),
+            *[pltpu.VMEM(e_field.shape, F32)] * 4,
             pltpu.VMEM((cx, cy, nz), jnp.int32),
-            pltpu.VMEM((4, 2, cx, nz), F32),
+            pltpu.VMEM((2, 2, cy, nz), F32),
+            pltpu.VMEM((2, 2, 2, cx, nz), F32),
+            pltpu.VMEM((2, 2, 1, nz), F32),
+            pltpu.VMEM((2, 2, cy, nz), F32),
+            pltpu.VMEM((2, 2, cy, nz), F32),
             pltpu.VMEM((2, 2, cx, nz), F32),
             pltpu.VMEM((2, 2, cx, nz), F32),
+            pltpu.VMEM((2, 2, 1, nz), F32),
             pltpu.VMEM((2, 8, 128), F32),
             *[pltpu.SMEM(table.shape, F32) for table in (eps_table, delta_table, omega_table, damping_table)],
             pltpu.SMEM(surface_flags.shape, jnp.int32),
-            dma((10,)), dma((5,)), dma((4, 2 * (cy // BY))), dma((4, 2 * (cy // BY))), dma((4,)), dma((4,)),
+            dma((10,)), dma((5,)), *[dma((2, 2, 2 * (cy // BY)))] * 2, *[dma((2, 2))] * 4,
             dma((2, ngx * ngy)), dma((2, ngx * ngy)), pltpu.SemaphoreType.REGULAR,
         ],
         compiler_params=pltpu.CompilerParams(
@@ -539,7 +622,7 @@
       eps_table, delta_table, omega_table, damping_table, surface_flags)
 
     steps = (NDIR // 4) // TILE
-    seeds, tables = make_seeds(nx, ny), make_tables(ny, cy)
+    seeds = make_seeds(nx, ny)
     far, e, h, p = pl.pallas_call(
         functools.partial(far_kernel, ngx, ngy, nx, ny),
         grid=(steps,),
@@ -547,7 +630,6 @@
         in_specs=[
             pl.BlockSpec(g.shape, lambda i: (0, 0, 0, 0)),
             pl.BlockSpec((1, *seeds.shape[1:]), lambda i: (i, 0, 0)),
-            pl.BlockSpec((1, *tables.shape[1:]), lambda i: (i, 0, 0)),
             hbm, hbm, hbm,
         ],
         out_specs=(pl.BlockSpec((2, 2, 4, 4 * TILE), lambda i: (0, 0, 0, i)), hbm, hbm, hbm),
@@ -558,7 +640,7 @@
             dma((2, 3)),
         ],
         compiler_params=pltpu.CompilerParams(vmem_limit_bytes=56 * 1024 * 1024),
-    )(g, jnp.asarray(seeds), jnp.asarray(tables), e, h, p)
+    )(g, jnp.asarray(seeds), e, h, p)
     return e, h, p, far
 
 

time: 42.3 us -> 39.7 us (0.939)
  Pallas kernels: 40.8 us -> 38.3 us
    pallas_call x1, Pallas kernels: 10.2 us -> 8.66 us  [shards(): pl.pallas_call(functools.partial(far_kernel, ngx, ngy, nx, ny), grid=(ste...]
    pallas_call x1, Pallas kernels: 30.7 us -> 29.6 us  [shards(): pl.pallas_call(functools.partial(step_kernel, ngx, ngy, eps_table.shape[0...]
where the time goes in v2:
time: 39.7 us; the launch traced here: 39.6 us
  Pallas kernels  38.3 us (96%)
  between operations  1.29 us (3%)
    pallas_call x1, Pallas kernels, shards(): pl.pallas_call(functools.partial(step_kernel, ngx, ngy, eps_table.shape[0...  29.6 us
    pallas_call x1, Pallas kernels, shards(): pl.pallas_call(functools.partial(far_kernel, ngx, ngy, nx, ny), grid=(ste...  8.66 us

profile of v2, /device:TPU:0, one launch (start us, length us, event | category | flops | bytes accessed | tf_op | source)
XLA Modules:
  0.0 39.6 jit_solution(16314601112612998219)
XLA Ops:
  1.3 29.6 %shard_map.138 = (f32[3,8,32,512]{3,2,1,0:T(8,128)}, f32[3,8,32,512]{3,2,1,0:T(8,128)}, f32[3,8,32,512]{3,2,1,0:T(8,128)}, f32[2,32,8,128]{3,2,1,0:T(8,128)}) custom-call(f32[3,8,32,512]{3,2,1,0:T(8,128)} %e_in.1, f32[3,8,32,512]{3,2,1,0:T(8,128)} %h_in.1, f32[3,8,32,512]{3,2,1,0:T(8,128)} %p_in.1, f32[3,8,32,512]{3,2,1,0:T(8,128)} %q_in.1, ...), custom_call_target="tpu_custom_call" | custom-call | tf_op jit(solution)/shard_map/pallas_call | solution.py:597
  30.9 8.7 %shard_map.139 = (f32[2,2,4,16384]{3,2,1,0:T(4,128)}, f32[3,8,32,512]{3,2,1,0:T(8,128)}, f32[3,8,32,512]{3,2,1,0:T(8,128)}, f32[3,8,32,512]{3,2,1,0:T(8,128)}) custom-call(f32[2,32,8,128]{3,2,1,0:T(8,128)} %get-tuple-element.12.g_ref, f32[4,64,1024]{2,1,0:T(8,128)} %constant.2.clone.seeds, f32[3,8,32,512]{3,2,1,0:T(8,128)} %get-tuple-element.13.e_in, ...), custom_call_target="tpu_custom_call" | custom-call | tf_op jit(solution)/shard_map/pallas_call | solution.py:626

commit v3 on v2

--- a/solution.py
+++ b/solution.py
@@ -19,6 +19,8 @@
 F32 = jnp.float32
 BF16 = jnp.bfloat16
 BY = 8
+H_PARTS = (((128, 512), (0, 128)), ((256, 512), (0, 256)))
+E_PARTS = (((256, 512), (0, 256)), ((384, 512), (0, 384)))
 
 
 def coefficients(nmat, nz, eps, delta, omega, damping):
@@ -60,7 +62,7 @@
         pltpu.make_async_copy(damping_in, damping, in_sem.at[8]),
         pltpu.make_async_copy(flags_in, flags, in_sem.at[9]),
     ]
-    for load in loads:
+    for load in loads[:2] + loads[5:]:
         load.start()
 
     barrier = pltpu.get_barrier_semaphore()
@@ -95,175 +97,194 @@
     sends_x, takes_x = (not_low_x, not_high_x), (not_high_x, not_low_x)
     sends_y, takes_y = (not_low_y, not_high_y), (not_high_y, not_low_y)
 
-    def x_copies(step, way, block):
+    def lanes_of(step, way, part):
+        low, high = (H_PARTS, E_PARTS)[way][step][part]
+        return pl.ds(low, high - low)
+
+    def x_copies(step, way, part):
+        lanes = lanes_of(step, way, part)
         copies = []
         for i in range(2):
-            rows = pl.ds(block * BY, BY)
-            src = E.at[1 + i, 0, rows] if way == 0 else xstage.at[step, i, rows]
-            dst = (xe, xh)[way].at[step, i, rows]
-            sem = 2 * block + i
+            src = E.at[1 + i, 0, :, lanes] if way == 0 else xstage.at[step, i, :, lanes]
+            dst = (xe, xh)[way].at[step, i, :, lanes]
             copies.append(pltpu.make_async_remote_copy(
-                src_ref=src, dst_ref=dst, send_sem=xs_sem.at[step, way, sem], recv_sem=xr_sem.at[step, way, sem],
+                src_ref=src, dst_ref=dst,
+                send_sem=xs_sem.at[step, way, 2 * part + i], recv_sem=xr_sem.at[step, way, 2 * part + i],
                 device_id=(lax.rem(gx + (ngx - 1, 1)[way], ngx), gy), device_id_type=MESH))
         return copies
 
-    def y_copy(step, way):
+    def y_copy(step, way, part):
+        lanes = lanes_of(step, way, part)
         return pltpu.make_async_remote_copy(
-            src_ref=ystage.at[step, way], dst_ref=(ye, yh)[way].at[step],
-            send_sem=ys_sem.at[step, way], recv_sem=yr_sem.at[step, way],
+            src_ref=ystage.at[step, way, :, :, :, lanes], dst_ref=(ye, yh)[way].at[step, :, :, :, lanes],
+            send_sem=ys_sem.at[step, way, part], recv_sem=yr_sem.at[step, way, part],
             device_id=(gx, lax.rem(gy + (ngy - 1, 1)[way], ngy)), device_id_type=MESH)
 
     sends_c = (not_high_x & not_low_y, not_low_x & not_high_y)
     takes_c = (not_low_x & not_high_y, not_high_x & not_low_y)
 
-    def c_copy(step, kind):
+    def c_copy(step, kind, part):
         dx, dy = ((1, ngy - 1), (ngx - 1, 1))[kind]
+        lanes = lanes_of(step, 1, part)
         return pltpu.make_async_remote_copy(
-            src_ref=cstage.at[step, kind], dst_ref=ce.at[step, kind],
-            send_sem=cs_sem.at[step, kind], recv_sem=cr_sem.at[step, kind],
+            src_ref=cstage.at[step, kind, :, lanes], dst_ref=ce.at[step, kind, :, lanes],
+            send_sem=cs_sem.at[step, kind, part], recv_sem=cr_sem.at[step, kind, part],
             device_id=(lax.rem(gx + dx, ngx), lax.rem(gy + dy, ngy)), device_id_type=MESH)
 
-    def send_x(step, way, block):
+    def send_x(step, way, part):
         @pl.when(sends_x[way])
         def _():
-            for copy in x_copies(step, way, block):
+            for copy in x_copies(step, way, part):
                 copy.start()
 
-    def take_x(step, way, block):
+    def take_x(step, way, part):
         @pl.when(takes_x[way])
         def _():
-            for copy in x_copies(step, way, block):
+            for copy in x_copies(step, way, part):
                 copy.wait_recv()
 
-    def sent_x(step, way):
+    def sent_x(step, way, part):
         @pl.when(sends_x[way])
         def _():
-            for block in blocks:
-                for copy in x_copies(step, way, block):
-                    copy.wait_send()
-
-    def send_y(step, way):
-        pl.when(sends_y[way])(lambda: y_copy(step, way).start())
-
-    def take_y(step, way):
-        pl.when(takes_y[way])(lambda: y_copy(step, way).wait_recv())
-
-    def sent_y(step, way):
-        pl.when(sends_y[way])(lambda: y_copy(step, way).wait_send())
-
-    def send_c(step, kind):
-        if kind == 0:
-            cstage[step, 0] = E[0, cx - 1, 0:1, :]
-        else:
-            cstage[step, 1] = E[1, 0, cy - 1 : cy, :]
-        pl.when(sends_c[kind])(lambda: c_copy(step, kind).start())
-
-    def take_c(step, kind):
-        pl.when(takes_c[kind])(lambda: c_copy(step, kind).wait_recv())
-
-    def sent_c(step, kind):
-        pl.when(sends_c[kind])(lambda: c_copy(step, kind).wait_send())
+            for copy in x_copies(step, way, part):
+                copy.wait_send()
+
+    def send_y(step, way, part):
+        pl.when(sends_y[way])(lambda: y_copy(step, way, part).start())
+
+    def take_y(step, way, part):
+        pl.when(takes_y[way])(lambda: y_copy(step, way, part).wait_recv())
+
+    def sent_y(step, way, part):
+        pl.when(sends_y[way])(lambda: y_copy(step, way, part).wait_send())
+
+    def send_c(step, part):
+        lanes = slice(*E_PARTS[step][part])
+        cstage[step, 0, :, lanes] = E[0, cx - 1, 0:1, lanes]
+        cstage[step, 1, :, lanes] = E[1, 0, cy - 1 : cy, lanes]
+        for kind in range(2):
+            pl.when(sends_c[kind])(lambda: c_copy(step, kind, part).start())
+
+    def take_c(step, kind, part):
+        pl.when(takes_c[kind])(lambda: c_copy(step, kind, part).wait_recv())
+
+    def sent_c(step, kind, part):
+        pl.when(sends_c[kind])(lambda: c_copy(step, kind, part).wait_send())
 
     blocks = range(cy // BY)
     last = cy // BY - 1
 
-    row_id = lax.broadcasted_iota(jnp.int32, (BY, nz), 0)
-    lane_id = lax.broadcasted_iota(jnp.int32, (BY, nz), 1)
-
-    def up_y(v, row):
-        return jnp.where(row_id == BY - 1, row, pltpu.roll(v, BY - 1, 0))
-
-    def up_z(v):
-        return jnp.where(lane_id == nz - 1, 0.0, pltpu.roll(v, nz - 1, 1))
-
-    def down_y(v, row):
-        return jnp.where(row_id == 0, row, pltpu.roll(v, 1, 0))
-
-    def down_z(v):
-        return jnp.where(lane_id == 0, 0.0, pltpu.roll(v, 1, 1))
-
-    def part_x(step, block):
-        here, x, y = pl.ds(block * BY, BY), cx - 1, block * BY
-        ex, ey, ez = E[0, x, here, :], E[1, x, here, :], E[2, x, here, :]
-        rx = E[0, x, y + BY : y + BY + 1, :] if block < last else jnp.zeros((1, nz), F32)
-        xstage[step, 0, here, :] = H[1, x, here, :] - DT * ((up_z(ex) - ex) + ez)
-        xstage[step, 1, here, :] = H[2, x, here, :] + DT * (ey + (up_y(ex, rx) - ex))
-        send_x(step, 1, block)
-
-    def part_y(step):
-        here = pl.ds(cy - BY, BY)
+    def ids(span, dim):
+        return lax.broadcasted_iota(jnp.int32, (BY, span[1] - span[0]), dim)
+
+    def up_y(v, row, span):
+        return jnp.where(ids(span, 0) == BY - 1, row, pltpu.roll(v, BY - 1, 0))
+
+    def down_y(v, row, span):
+        return jnp.where(ids(span, 0) == 0, row, pltpu.roll(v, 1, 0))
+
+    def up_z(ref, c, x, here, span):
+        low, high = span
+        n = high - low
+        if high == nz:
+            return jnp.where(ids(span, 1) == n - 1, 0.0, pltpu.roll(ref[c, x, here, low:high], n - 1, 1))
+        return pltpu.roll(ref[c, x, here, low : high + 128], n + 127, 1)[:, :n]
+
+    def down_z(ref, c, x, here, span):
+        low, high = span
+        if low == 0:
+            return jnp.where(ids(span, 1) == 0, 0.0, pltpu.roll(ref[c, x, here, low:high], 1, 1))
+        return pltpu.roll(ref[c, x, here, low - 128 : high], 1, 1)[:, 128:]
+
+    def part_x(step, part):
+        span = E_PARTS[step][part]
+        lanes, x = slice(*span), cx - 1
+        for block in blocks:
+            here, y = pl.ds(block * BY, BY), block * BY
+            ex, ey, ez = E[0, x, here, lanes], E[1, x, here, lanes], E[2, x, here, lanes]
+            rx = E[0, x, y + BY : y + BY + 1, lanes] if block < last else jnp.zeros((1, span[1] - span[0]), F32)
+            xstage[step, 0, here, lanes] = H[1, x, here, lanes] - DT * ((up_z(E, 0, x, here, span) - ex) + ez)
+            xstage[step, 1, here, lanes] = H[2, x, here, lanes] + DT * (ey + (up_y(ex, rx, span) - ex))
+        send_x(step, 1, part)
+
+    def part_y(step, part):
+        span = E_PARTS[step][part]
+        here, lanes = pl.ds(cy - BY, BY), slice(*span)
         for x in range(cx):
-            ex, ey, ez = E[0, x, here, :], E[1, x, here, :], E[2, x, here, :]
-            slope = E[1, x + 1, here, :] - ey if x < cx - 1 else -ey
-            part_hx = H[0, x, here, :] + DT * (ez + (up_z(ey) - ey))
-            part_hz = H[2, x, here, :] - DT * (slope + ex)
-            ystage[step, 1, 0, x : x + 1, :] = part_hx[BY - 1 : BY, :]
-            ystage[step, 1, 1, x : x + 1, :] = part_hz[BY - 1 : BY, :]
-        send_y(step, 1)
-
-    def rows_y(step):
+            ex, ey, ez = E[0, x, here, lanes], E[1, x, here, lanes], E[2, x, here, lanes]
+            slope = E[1, x + 1, here, lanes] - ey if x < cx - 1 else -ey
+            part_hx = H[0, x, here, lanes] + DT * (ez + (up_z(E, 1, x, here, span) - ey))
+            part_hz = H[2, x, here, lanes] - DT * (slope + ex)
+            ystage[step, 1, 0, x, :, lanes] = part_hx[BY - 1 : BY, :]
+            ystage[step, 1, 1, x, :, lanes] = part_hz[BY - 1 : BY, :]
+        send_y(step, 1, part)
+
+    def rows_y(step, part):
+        lanes = slice(*H_PARTS[step][part])
         for i, c in enumerate((0, 2)):
             for x in range(cx):
-                ystage[step, 0, i, x : x + 1, :] = E[c, x, 0:1, :]
-        send_y(step, 0)
-
-    def h_plane(step, x, blocks):
+                ystage[step, 0, i, x, :, lanes] = E[c, x, 0:1, lanes]
+        send_y(step, 0, part)
+
+    def h_plane(step, x, blocks, span):
+        lanes = slice(*span)
         for y in [BY * block for block in blocks]:
             here = pl.ds(y, BY)
-            ex, ey, ez = E[0, x, here, :], E[1, x, here, :], E[2, x, here, :]
+            ex, ey, ez = E[0, x, here, lanes], E[1, x, here, lanes], E[2, x, here, lanes]
             if y + BY < cy:
-                rx, rz = E[0, x, y + BY : y + BY + 1, :], E[2, x, y + BY : y + BY + 1, :]
+                rx, rz = E[0, x, y + BY : y + BY + 1, lanes], E[2, x, y + BY : y + BY + 1, lanes]
             else:
-                rx, rz = ye[step, 0, pl.ds(x, 1), :], ye[step, 1, pl.ds(x, 1), :]
+                rx, rz = ye[step, 0, x, :, lanes], ye[step, 1, x, :, lanes]
             if isinstance(x, int) and x == cx - 1:
-                eyx, ezx = xe[step, 0, here, :], xe[step, 1, here, :]
+                eyx, ezx = xe[step, 0, here, lanes], xe[step, 1, here, lanes]
             else:
-                eyx, ezx = E[1, x + 1, here, :], E[2, x + 1, here, :]
-            curl_x = (up_y(ez, rz) - ez) - (up_z(ey) - ey)
-            curl_y = (up_z(ex) - ex) - (ezx - ez)
-            curl_z = (eyx - ey) - (up_y(ex, rx) - ex)
-            H[0, x, here, :] = H[0, x, here, :] - DT * curl_x
-            H[1, x, here, :] = H[1, x, here, :] - DT * curl_y
-            H[2, x, here, :] = H[2, x, here, :] - DT * curl_z
-
-    def e_plane(step, x, coef, blocks):
+                eyx, ezx = E[1, x + 1, here, lanes], E[2, x + 1, here, lanes]
+            curl_x = (up_y(ez, rz, span) - ez) - (up_z(E, 1, x, here, span) - ey)
+            curl_y = (up_z(E, 0, x, here, span) - ex) - (ezx - ez)
+            curl_z = (eyx - ey) - (up_y(ex, rx, span) - ex)
+            H[0, x, here, lanes] = H[0, x, here, lanes] - DT * curl_x
+            H[1, x, here, lanes] = H[1, x, here, lanes] - DT * curl_y
+            H[2, x, here, lanes] = H[2, x, here, lanes] - DT * curl_z
+
+    def e_plane(step, x, coef, blocks, span):
         now, old = (PA, PB) if step == 0 else (PB, PA)
         fixed = isinstance(x, int)
+        lanes, n = slice(*span), span[1] - span[0]
         for y in [BY * block for block in blocks]:
             here = pl.ds(y, BY)
-            mat = MAT[x, here, :]
-            vox = [jnp.broadcast_to(coef[nmat - 1][i], (BY, nz)) for i in range(4)]
+            mat = MAT[x, here, lanes]
+            vox = [jnp.broadcast_to(coef[nmat - 1][i][:, :n], (BY, n)) for i in range(4)]
             for m in range(nmat - 1):
                 hit = mat == m
-                vox = [jnp.where(hit, coef[m][i], vox[i]) for i in range(4)]
+                vox = [jnp.where(hit, coef[m][i][:, :n], vox[i]) for i in range(4)]
             a, b, c, inv = vox
-            hx, hy, hz = H[0, x, here, :], H[1, x, here, :], H[2, x, here, :]
+            hx, hy, hz = H[0, x, here, lanes], H[1, x, here, lanes], H[2, x, here, lanes]
             if y > 0:
-                rx, rz = H[0, x, y - 1 : y, :], H[2, x, y - 1 : y, :]
+                rx, rz = H[0, x, y - 1 : y, lanes], H[2, x, y - 1 : y, lanes]
             else:
-                rx = yh[step, 0, pl.ds(x, 1), :] - dt_y * E[2, x, 0:1, :]
-                edge = E[0, x, 0:1, :]
+                rx = yh[step, 0, x, :, lanes] - dt_y * E[2, x, 0:1, lanes]
+                edge = E[0, x, 0:1, lanes]
                 if fixed and x == cx - 1:
-                    edge = edge - ce[step, 1]
-                rz = yh[step, 1, pl.ds(x, 1), :] + dt_y * edge
+                    edge = edge - ce[step, 1, :, lanes]
+                rz = yh[step, 1, x, :, lanes] + dt_y * edge
             if fixed and x == 0:
-                hyx = xh[step, 0, here, :] + dt_x * E[2, 0, here, :]
-                edge = E[1, 0, here, :]
+                hyx = xh[step, 0, here, lanes] + dt_x * E[2, 0, here, lanes]
+                edge = E[1, 0, here, lanes]
                 if y + BY == cy:
-                    edge = jnp.where(row_id == BY - 1, edge - ce[step, 0], edge)
-                hzx = xh[step, 1, here, :] - dt_x * edge
+                    edge = jnp.where(ids(span, 0) == BY - 1, edge - ce[step, 0, :, lanes], edge)
+                hzx = xh[step, 1, here, lanes] - dt_x * edge
             else:
-                hyx, hzx = H[1, x - 1, here, :], H[2, x - 1, here, :]
+                hyx, hzx = H[1, x - 1, here, lanes], H[2, x - 1, here, lanes]
             curls = (
-                (hz - down_y(hz, rz)) - (hy - down_z(hy)),
-                (hx - down_z(hx)) - (hz - hzx),
-                (hy - hyx) - (hx - down_y(hx, rx)),
+                (hz - down_y(hz, rz, span)) - (hy - down_z(H, 1, x, here, span)),
+                (hx - down_z(H, 0, x, here, span)) - (hz - hzx),
+                (hy - hyx) - (hx - down_y(hx, rx, span)),
             )
             for i in range(3):
-                e, p = E[i, x, here, :], now[i, x, here, :]
-                new = a * p + b * old[i, x, here, :] + c * e
-                E[i, x, here, :] = e + (DT * curls[i] - (new - p)) * inv
-                old[i, x, here, :] = new
+                e, p = E[i, x, here, lanes], now[i, x, here, lanes]
+                new = a * p + b * old[i, x, here, lanes] + c * e
+                E[i, x, here, lanes] = e + (DT * curls[i] - (new - p)) * inv
+                old[i, x, here, lanes] = new
 
     me = gx * ngy + gy
     count = ngx * ngy
@@ -314,17 +335,22 @@
         def _(k):
             peer(step, k).wait()
 
+    every = (0, nz)
     loads[0].wait()
     pl.semaphore_wait(barrier, ngx + ngy)
     send_c(0, 0)
+    send_x(0, 0, 0)
+    rows_y(0, 0)
+    loads[1].wait()
+    for load in loads[2:5]:
+        load.start()
+    part_x(0, 0)
+    part_y(0, 0)
     send_c(0, 1)
-    for block in blocks:
-        send_x(0, 0, block)
-    rows_y(0)
-    loads[1].wait()
-    for block in blocks:
-        part_x(0, block)
-    part_y(0)
+    send_x(0, 0, 1)
+    rows_y(0, 1)
+    part_x(0, 1)
+    part_y(0, 1)
     for k in range(1, ngy):
         pl.semaphore_signal(all_in, inc=1, device_id=(gx, lax.rem(gy + k, ngy)), device_id_type=MESH)
     for load in loads[5:]:
@@ -337,7 +363,7 @@
 
         @pl.loop(0, cx - 1)
         def _(x):
-            h_plane(step, x, range(last))
+            h_plane(step, x, range(last), every)
 
         if step == 0:
             for load in loads[2:5]:
@@ -347,52 +373,46 @@
 
         @pl.loop(1, cx - 1)
         def _(x):
-            e_plane(step, x, coef, range(1, last))
-
-        for block in range(last):
-            take_x(step, 0, block)
-            h_plane(step, cx - 1, [block])
-        take_y(step, 0)
-        take_x(step, 0, last)
-        h_plane(step, cx - 1, [last])
-
-        @pl.loop(0, cx - 1)
-        def _(x):
-            h_plane(step, x, [last])
-
-        if step == 1:
-            pltpu.make_async_copy(H, h_out, out_sem.at[0]).start()
-        sent_x(step, 0)
-        take_y(step, 1)
-        take_c(step, 1)
-        for block in range(last, -1, -1):
-            e_plane(step, cx - 1, coef, [block])
+            e_plane(step, x, coef, range(1, last), every)
+
+        for part in range(2):
+            h_span, e_span = H_PARTS[step][part], E_PARTS[step][part]
+            take_y(step, 0, part)
+
+            @pl.loop(0, cx - 1)
+            def _(x):
+                h_plane(step, x, [last], h_span)
+
+            take_x(step, 0, part)
+            h_plane(step, cx - 1, blocks, h_span)
+            if step == 1 and part == 1:
+                pltpu.make_async_copy(H, h_out, out_sem.at[0]).start()
+            sent_x(step, 0, part)
+            take_y(step, 1, part)
+            take_c(step, 1, part)
+            e_plane(step, cx - 1, coef, blocks, e_span)
             if step == 0:
-                part_x(1, block)
+                part_x(1, part)
+            take_x(step, 1, part)
+            take_c(step, 0, part)
+            e_plane(step, 0, coef, blocks, e_span)
+            if step == 0:
+                send_x(1, 0, part)
+                send_c(1, part)
+
+            @pl.loop(1, cx - 1)
+            def _(x):
+                e_plane(step, x, coef, [0, last], e_span)
+
+            if step == 0:
+                rows_y(1, part)
+                part_y(1, part)
+            elif part == 0:
+                surface(1, flag)
+                gather_start(1)
         if step == 0:
-            send_c(1, 0)
-        for block in blocks:
-            take_x(step, 1, block)
-            if block == last:
-                take_c(step, 0)
-            e_plane(step, 0, coef, [block])
-            if step == 0:
-                send_x(1, 0, block)
-        if step == 0:
-            send_c(1, 1)
-
-        @pl.loop(1, cx - 1)
-        def _(x):
-            e_plane(step, x, coef, [0, last])
-
-        if step == 0:
-            rows_y(1)
-            part_y(1)
-        surface(step, flag)
-        if step == 0:
+            surface(0, flag)
             pl.semaphore_wait(all_in, ngy - 1)
-        else:
-            gather_start(1)
 
     saves = [
         pltpu.make_async_copy(H, h_out, out_sem.at[0]),
@@ -402,10 +422,11 @@
     saves[1].start()
     saves[2].start()
     for step in range(2):
-        sent_x(step, 1)
-        for i in range(2):
-            sent_y(step, i)
-            sent_c(step, i)
+        for part in range(2):
+            sent_x(step, 1, part)
+            for i in range(2):
+                sent_y(step, i, part)
+                sent_c(step, i, part)
     gather_end(0)
     gather_end(1)
     for save in saves:
@@ -603,17 +624,17 @@
             *[pltpu.VMEM(e_field.shape, F32)] * 4,
             pltpu.VMEM((cx, cy, nz), jnp.int32),
             pltpu.VMEM((2, 2, cy, nz), F32),
-            pltpu.VMEM((2, 2, 2, cx, nz), F32),
+            pltpu.VMEM((2, 2, 2, cx, 1, nz), F32),
             pltpu.VMEM((2, 2, 1, nz), F32),
             pltpu.VMEM((2, 2, cy, nz), F32),
             pltpu.VMEM((2, 2, cy, nz), F32),
-            pltpu.VMEM((2, 2, cx, nz), F32),
-            pltpu.VMEM((2, 2, cx, nz), F32),
+            pltpu.VMEM((2, 2, cx, 1, nz), F32),
+            pltpu.VMEM((2, 2, cx, 1, nz), F32),
             pltpu.VMEM((2, 2, 1, nz), F32),
             pltpu.VMEM((2, 8, 128), F32),
             *[pltpu.SMEM(table.shape, F32) for table in (eps_table, delta_table, omega_table, damping_table)],
             pltpu.SMEM(surface_flags.shape, jnp.int32),
-            dma((10,)), dma((5,)), *[dma((2, 2, 2 * (cy // BY)))] * 2, *[dma((2, 2))] * 4,
+            dma((10,)), dma((5,)), *[dma((2, 2, 4))] * 2, *[dma((2, 2, 2))] * 4,
             dma((2, ngx * ngy)), dma((2, ngx * ngy)), pltpu.SemaphoreType.REGULAR,
         ],
         compiler_params=pltpu.CompilerParams(

time: 39.7 us -> 35.8 us (0.902)
  Pallas kernels: 38.3 us -> 34.3 us
    pallas_call x1, Pallas kernels: 29.6 us -> 25.6 us  [shards(): pl.pallas_call(functools.partial(step_kernel, ngx, ngy, eps_table.shape[0...]
where the time goes in v3:
time: 35.8 us; the launch traced here: 35.6 us
  Pallas kernels  34.3 us (96%)
  between operations  1.29 us (4%)
    pallas_call x1, Pallas kernels, shards(): pl.pallas_call(functools.partial(step_kernel, ngx, ngy, eps_table.shape[0...  25.6 us
    pallas_call x1, Pallas kernels, shards(): pl.pallas_call(functools.partial(far_kernel, ngx, ngy, nx, ny), grid=(ste...  8.68 us

profile of v3, /device:TPU:0, one launch (start us, length us, event | category | flops | bytes accessed | tf_op | source)
XLA Modules:
  0.0 35.6 jit_solution(3785515790283990707)
XLA Ops:
  1.3 25.6 %shard_map.138 = (f32[3,8,32,512]{3,2,1,0:T(8,128)}, f32[3,8,32,512]{3,2,1,0:T(8,128)}, f32[3,8,32,512]{3,2,1,0:T(8,128)}, f32[2,32,8,128]{3,2,1,0:T(8,128)}) custom-call(f32[3,8,32,512]{3,2,1,0:T(8,128)} %e_in.1, f32[3,8,32,512]{3,2,1,0:T(8,128)} %h_in.1, f32[3,8,32,512]{3,2,1,0:T(8,128)} %p_in.1, f32[3,8,32,512]{3,2,1,0:T(8,128)} %q_in.1, ...), custom_call_target="tpu_custom_call" | custom-call | tf_op jit(solution)/shard_map/pallas_call | solution.py:618
  26.9 8.7 %shard_map.139 = (f32[2,2,4,16384]{3,2,1,0:T(4,128)}, f32[3,8,32,512]{3,2,1,0:T(8,128)}, f32[3,8,32,512]{3,2,1,0:T(8,128)}, f32[3,8,32,512]{3,2,1,0:T(8,128)}) custom-call(f32[2,32,8,128]{3,2,1,0:T(8,128)} %get-tuple-element.12.g_ref, f32[4,64,1024]{2,1,0:T(8,128)} %constant.2.clone.seeds, f32[3,8,32,512]{3,2,1,0:T(8,128)} %get-tuple-element.13.e_in, ...), custom_call_target="tpu_custom_call" | custom-call | tf_op jit(solution)/shard_map/pallas_call | solution.py:647

commit v4 on v3

--- a/solution.py
+++ b/solution.py
@@ -50,19 +50,15 @@
     gx = lax.axis_index("gx")
     gy = lax.axis_index("gy")
 
-    loads = [
-        pltpu.make_async_copy(e_in, E, in_sem.at[0]),
-        pltpu.make_async_copy(h_in, H, in_sem.at[1]),
-        pltpu.make_async_copy(p_in, PA, in_sem.at[2]),
-        pltpu.make_async_copy(q_in, PB, in_sem.at[3]),
-        pltpu.make_async_copy(m_in, MAT, in_sem.at[4]),
-        pltpu.make_async_copy(eps_in, eps, in_sem.at[5]),
-        pltpu.make_async_copy(delta_in, delta, in_sem.at[6]),
-        pltpu.make_async_copy(omega_in, omega, in_sem.at[7]),
-        pltpu.make_async_copy(damping_in, damping, in_sem.at[8]),
-        pltpu.make_async_copy(flags_in, flags, in_sem.at[9]),
+    inner, lower = pl.ds(1, cx - 2), pl.ds(0, cx - 1)
+    pairs = [
+        (e_in.at[:, 0], E.at[:, 0]), (e_in.at[:, cx - 1], E.at[:, cx - 1]), (h_in.at[:, cx - 1], H.at[:, cx - 1]),
+        (e_in.at[:, inner], E.at[:, inner]), (h_in.at[:, lower], H.at[:, lower]),
+        (p_in, PA), (q_in, PB), (m_in, MAT),
+        (eps_in, eps), (delta_in, delta), (omega_in, omega), (damping_in, damping), (flags_in, flags),
     ]
-    for load in loads[:2] + loads[5:]:
+    loads = [pltpu.make_async_copy(src, dst, in_sem.at[i]) for i, (src, dst) in enumerate(pairs)]
+    for load in loads[:5] + loads[8:]:
         load.start()
 
     barrier = pltpu.get_barrier_semaphore()
@@ -324,8 +320,7 @@
     def gather_start(step):
         own(step).start()
 
-        @pl.loop(1, count)
-        def _(k):
+        for k in range(1, count):
             peer(step, k).start()
 
     def gather_end(step):
@@ -338,22 +333,25 @@
     every = (0, nz)
     loads[0].wait()
     pl.semaphore_wait(barrier, ngx + ngy)
+    send_x(0, 0, 0)
+    loads[1].wait()
     send_c(0, 0)
-    send_x(0, 0, 0)
+    loads[2].wait()
+    part_x(0, 0)
+    send_x(0, 0, 1)
+    loads[3].wait()
     rows_y(0, 0)
-    loads[1].wait()
-    for load in loads[2:5]:
+    loads[4].wait()
+    for load in loads[5:8]:
         load.start()
-    part_x(0, 0)
     part_y(0, 0)
     send_c(0, 1)
-    send_x(0, 0, 1)
+    part_x(0, 1)
     rows_y(0, 1)
-    part_x(0, 1)
     part_y(0, 1)
     for k in range(1, ngy):
         pl.semaphore_signal(all_in, inc=1, device_id=(gx, lax.rem(gy + k, ngy)), device_id_type=MESH)
-    for load in loads[5:]:
+    for load in loads[8:]:
         load.wait()
 
     coef = coefficients(nmat, nz, eps, delta, omega, damping)
@@ -366,7 +364,7 @@
             h_plane(step, x, range(last), every)
 
         if step == 0:
-            for load in loads[2:5]:
+            for load in loads[5:8]:
                 load.wait()
         else:
             gather_start(0)
@@ -464,55 +462,57 @@
 
 
 def far_kernel(
-    ngx, ngy, nx, ny, g_ref, seeds, e_in, h_in, p_in, far, e_out, h_out, p_out,
-    a_high, a_low, e_pass, h_pass, p_pass, sem,
+    ngx, ngy, nx, ny, g_in, seeds_in, e_in, h_in, p_in, far_out, e_out, h_out, p_out,
+    g_ref, seeds, far, a_high, a_low, e_pass, h_pass, p_pass, sem, seed_sem, far_sem, g_sem,
 ):
-    pid = pl.program_id(0)
     half = 2 * nx
     depth = ny // 2
     per = ny // ngy // 8
+    tiles = seeds.shape[0]
+    g_load = pltpu.make_async_copy(g_in, g_ref, g_sem)
+    g_load.start()
+
+    def seed_load(tile):
+        return pltpu.make_async_copy(seeds_in.at[tile], seeds.at[tile], seed_sem.at[tile])
+
+    def far_save(tile):
+        lanes = pl.ds(pl.multiple_of(tile * 4 * TILE, 4 * TILE), 4 * TILE)
+        return pltpu.make_async_copy(far.at[tile], far_out.at[:, :, :, lanes], far_sem.at[tile])
+
+    for tile in range(tiles):
+        seed_load(tile).start()
     fields = enumerate(zip((e_in, h_in, p_in), (e_pass, h_pass, p_pass), (e_out, h_out, p_out)))
     moves = [
         (pltpu.make_async_copy(src, mid, sem.at[0, i]), pltpu.make_async_copy(mid, dst, sem.at[1, i]))
         for i, (src, mid, dst) in fields
     ]
-
-    @pl.when(pid == 0)
-    def _():
-        for load, _ in moves:
-            load.start()
-        quarter = lax.broadcasted_iota(jnp.int32, (32, 128), 1) // 32
-        for s in range(2):
-            for x in range(ngx // 2):
-                for group in range(ngy // 8):
-                    kinds = [[], [], [], []]
-                    for y in range(4 * group, 4 * group + 4):
-                        low_x, high_x = x * ngy, (ngx - 1 - x) * ngy
-                        t00, t10 = g_ref[s, low_x + y], g_ref[s, high_x + y]
-                        t01, t11 = g_ref[s, low_x + ngy - 1 - y], g_ref[s, high_x + ngy - 1 - y]
-                        even0, even1, odd0, odd1 = t10 + t00, t11 + t01, t10 - t00, t11 - t01
-                        for kind, tile in zip(kinds, (even0 + even1, odd0 + odd1, even1 - even0, odd1 - odd0)):
-                            kind.append(tile)
-                    turned = jnp.concatenate(kinds[0] + kinds[1] + kinds[2] + kinds[3], axis=0).T
-                    for kind in range(4):
-                        block = jnp.zeros((32, 128), F32)
-                        for yb in range(4):
-                            piece = turned[32 * yb : 32 * yb + 32, :]
-                            shift = (32 * (yb - kind)) % 128
-                            if shift:
-                                piece = pltpu.roll(piece, shift, 1)
-                            block = jnp.where(quarter == yb, piece, block)
-                        high = block.astype(BF16)
-                        rows = pl.ds((2 * s + kind % 2) * half + 32 * x, 32)
-                        lanes = pl.ds(128 * group, 128)
-                        a_high[kind // 2, rows, lanes] = high
-                        a_low[kind // 2, rows, lanes] = (block - high.astype(F32)).astype(BF16)
-
-    @pl.when(pid == 1)
-    def _():
-        for load, save in moves:
-            load.wait()
-            save.start()
+    g_load.wait()
+    quarter = lax.broadcasted_iota(jnp.int32, (32, 128), 1) // 32
+    for s in range(2):
+        for x in range(ngx // 2):
+            for group in range(ngy // 8):
+                kinds = [[], [], [], []]
+                for y in range(4 * group, 4 * group + 4):
+                    low_x, high_x = x * ngy, (ngx - 1 - x) * ngy
+                    t00, t10 = g_ref[s, low_x + y], g_ref[s, high_x + y]
+                    t01, t11 = g_ref[s, low_x + ngy - 1 - y], g_ref[s, high_x + ngy - 1 - y]
+                    even0, even1, odd0, odd1 = t10 + t00, t11 + t01, t10 - t00, t11 - t01
+                    for kind, tile in zip(kinds, (even0 + even1, odd0 + odd1, even1 - even0, odd1 - odd0)):
+                        kind.append(tile)
+                turned = jnp.concatenate(kinds[0] + kinds[1] + kinds[2] + kinds[3], axis=0).T
+                for kind in range(4):
+                    block = jnp.zeros((32, 128), F32)
+                    for yb in range(4):
+                        piece = turned[32 * yb : 32 * yb + 32, :]
+                        shift = (32 * (yb - kind)) % 128
+                        if shift:
+                            piece = pltpu.roll(piece, shift, 1)
+                        block = jnp.where(quarter == yb, piece, block)
+                    high = block.astype(BF16)
+                    rows = pl.ds((2 * s + kind % 2) * half + 32 * x, 32)
+                    lanes = pl.ds(128 * group, 128)
+                    a_high[kind // 2, rows, lanes] = high
+                    a_low[kind // 2, rows, lanes] = (block - high.astype(F32)).astype(BF16)
 
     scale = 1.0 / math.sqrt(nx * ny)
     sub = lax.broadcasted_iota(jnp.int32, (8, PART), 0)
@@ -524,84 +524,102 @@
     def times(a, b):
         return (a[0] * b[0] - a[1] * b[1], a[0] * b[1] + a[1] * b[0])
 
-    for o in range(0, TILE, PART):
-        lanes = slice(o, o + PART)
-        for f in range(2):
-            omega = 2.0 * math.pi / WAVELENGTHS[f]
-            kappa = [math.cos(omega * (s + 1) * DT) * scale for s in range(2)]
-            sigma = [math.sin(omega * (s + 1) * DT) * scale for s in range(2)]
-
-            def seed(i):
-                row = 32 * f + 16 + i
-                return jnp.broadcast_to(seeds[0, row : row + 1, lanes], (8, PART))
-
-            v = (seeds[0, 32 * f : 32 * f + 8, lanes], seeds[0, 32 * f + 8 : 32 * f + 16, lanes])
-            e16 = (seed(12), seed(13))
-            w = times(v, (seed(10), seed(11)))
-            waves = []
-            for j in range(depth // 16):
-                waves += [v, w]
-                if 16 * (j + 1) < depth:
-                    v, w = times(v, e16), times(w, e16)
-            order = [
-                (4 * group + y) * per + yb for group in range(depth // 128) for yb in range(per) for y in range(4)
-            ]
-            sums = []
-            for trig in range(2):
-                full = jnp.concatenate([waves[j][trig] for j in order], axis=0)
-                high = full.astype(BF16)
-                low = (full - high.astype(F32)).astype(BF16)
-                ah, al = a_high[trig], a_low[trig]
-                sums.append(jnp.dot(
-                    jnp.concatenate([ah, ah, al], axis=1), jnp.concatenate([high, low, high], axis=0),
-                    preferred_element_type=F32))
-            w = (jnp.where(top, seed(0), seed(2)), jnp.where(top, seed(1), seed(3)))
-            e2 = (seed(4), seed(5))
-            acc = [[None] * 4, [None] * 4]
-            for g in range(nx // 4):
-                for s in range(2):
-                    for trig in range(2):
-                        for odd in range(2):
-                            at = (2 * s + odd) * half + 8 * g
-                            term = sums[trig][at : at + 8, :] * w[odd]
-                            i = 2 * trig + odd
-                            acc[s][i] = term if g == 0 else acc[s][i] + term
-                if g + 1 < nx // 4:
-                    w = times(w, e2)
-            ck, sk, dk, rk = [acc[0][i] * kappa[0] + acc[1][i] * kappa[1] for i in range(4)]
-            cg, sg, dg, rg = [acc[0][i] * sigma[0] + acc[1][i] * sigma[1] for i in range(4)]
-            re_same, re_diff = ck - rk, ck + rk
-            im_same, im_diff = cg - rg, cg + rg
-            plus_k, minus_k = sk + dk, sk - dk
-            plus_g, minus_g = sg + dg, sg - dg
-            quads = (
-                (re_same + plus_g, plus_k - im_same),
-                (re_diff - minus_g, -minus_k - im_diff),
-                (re_same - plus_g, -plus_k - im_same),
-                (re_diff + minus_g, minus_k - im_diff),
-            )
-            same = (seed(6), jnp.where(top, -seed(7), seed(7)))
-            diff = (seed(8), jnp.where(top, -seed(9), seed(9)))
-            done = []
-            for q, (re, im) in enumerate(quads):
-                both = jnp.where(top, re, im) + pltpu.roll(jnp.where(top, im, re), 4, 0)
-                turn = (same, diff)[q % 2]
-                swing = pltpu.roll(both, 4, 0) * turn[1]
-                done.append(both * turn[0] + (swing if q in (0, 3) else -swing))
-            for pair in range(PART // 128):
-                cut = slice(128 * pair, 128 * pair + 128)
-                for h in range(2):
-                    here, back = done[2 * h][:, cut], jnp.take_along_axis(done[2 * h + 1][:, cut], mirror, axis=1)
-                    both = (jnp.where(first, here, back), pltpu.roll(jnp.where(first, back, here), 64, 1))
-                    for t in range(2):
-                        d = (2 * (o // 128 + pair) + t) * 256 + h * 128
-                        far[f, 0, :, d : d + 128] = both[t][0:4]
-                        far[f, 1, :, d : d + 128] = both[t][4:8]
-
-    @pl.when(pid == pl.num_programs(0) - 1)
-    def _():
-        for _, save in moves:
-            save.wait()
+    @pl.loop(0, tiles)
+    def _(tile):
+        seed_load(tile).wait()
+
+        @pl.when(tile == 0)
+        def _():
+            for load, _ in moves:
+                load.start()
+
+        @pl.when(tile == 2)
+        def _():
+            for load, save in moves:
+                load.wait()
+                save.start()
+
+        for o in range(0, TILE, PART):
+            lanes = slice(o, o + PART)
+            for f in range(2):
+                omega = 2.0 * math.pi / WAVELENGTHS[f]
+                kappa = [math.cos(omega * (s + 1) * DT) * scale for s in range(2)]
+                sigma = [math.sin(omega * (s + 1) * DT) * scale for s in range(2)]
+
+                def seed(i):
+                    row = 32 * f + 16 + i
+                    return jnp.broadcast_to(seeds[tile, row : row + 1, lanes], (8, PART))
+
+                v = (seeds[tile, 32 * f : 32 * f + 8, lanes], seeds[tile, 32 * f + 8 : 32 * f + 16, lanes])
+                e16 = (seed(12), seed(13))
+                w = times(v, (seed(10), seed(11)))
+                waves = []
+                for j in range(depth // 16):
+                    waves += [v, w]
+                    if 16 * (j + 1) < depth:
+                        v, w = times(v, e16), times(w, e16)
+                order = [
+                    (4 * group + y) * per + yb for group in range(depth // 128) for yb in range(per) for y in range(4)
+                ]
+                sums = []
+                for trig in range(2):
+                    full = jnp.concatenate([waves[j][trig] for j in order], axis=0)
+                    high = full.astype(BF16)
+                    low = (full - high.astype(F32)).astype(BF16)
+                    ah, al = a_high[trig], a_low[trig]
+                    sums.append(jnp.dot(
+                        jnp.concatenate([ah, ah, al], axis=1), jnp.concatenate([high, low, high], axis=0),
+                        preferred_element_type=F32))
+                w = (jnp.where(top, seed(0), seed(2)), jnp.where(top, seed(1), seed(3)))
+                e2 = (seed(4), seed(5))
+                acc = [[None] * 4, [None] * 4]
+                for g in range(nx // 4):
+                    for s in range(2):
+                        for trig in range(2):
+                            for odd in range(2):
+                                at = (2 * s + odd) * half + 8 * g
+                                term = sums[trig][at : at + 8, :] * w[odd]
+                                i = 2 * trig + odd
+                                acc[s][i] = term if g == 0 else acc[s][i] + term
+                    if g + 1 < nx // 4:
+                        w = times(w, e2)
+                ck, sk, dk, rk = [acc[0][i] * kappa[0] + acc[1][i] * kappa[1] for i in range(4)]
+                cg, sg, dg, rg = [acc[0][i] * sigma[0] + acc[1][i] * sigma[1] for i in range(4)]
+                re_same, re_diff = ck - rk, ck + rk
+                im_same, im_diff = cg - rg, cg + rg
+                plus_k, minus_k = sk + dk, sk - dk
+                plus_g, minus_g = sg + dg, sg - dg
+                quads = (
+                    (re_same + plus_g, plus_k - im_same),
+                    (re_diff - minus_g, -minus_k - im_diff),
+                    (re_same - plus_g, -plus_k - im_same),
+                    (re_diff + minus_g, minus_k - im_diff),
+                )
+                same = (seed(6), jnp.where(top, -seed(7), seed(7)))
+                diff = (seed(8), jnp.where(top, -seed(9), seed(9)))
+                done = []
+                for q, (re, im) in enumerate(quads):
+                    both = jnp.where(top, re, im) + pltpu.roll(jnp.where(top, im, re), 4, 0)
+                    turn = (same, diff)[q % 2]
+                    swing = pltpu.roll(both, 4, 0) * turn[1]
+                    done.append(both * turn[0] + (swing if q in (0, 3) else -swing))
+                for pair in range(PART // 128):
+                    cut = slice(128 * pair, 128 * pair + 128)
+                    for h in range(2):
+                        here, back = done[2 * h][:, cut], jnp.take_along_axis(done[2 * h + 1][:, cut], mirror, axis=1)
+                        both = (jnp.where(first, here, back), pltpu.roll(jnp.where(first, back, here), 64, 1))
+                        for t in range(2):
+                            d = (2 * (o // 128 + pair) + t) * 256 + h * 128
+                            far[tile, f, 0, :, d : d + 128] = both[t][0:4]
+                            far[tile, f, 1, :, d : d + 128] = both[t][4:8]
+        far_save(tile).start()
+
+    @pl.loop(0, tiles)
+    def _(tile):
+        far_save(tile).wait()
+
+    for _, save in moves:
+        save.wait()
 
 
 def shards(
@@ -634,7 +652,7 @@
             pltpu.VMEM((2, 8, 128), F32),
             *[pltpu.SMEM(table.shape, F32) for table in (eps_table, delta_table, omega_table, damping_table)],
             pltpu.SMEM(surface_flags.shape, jnp.int32),
-            dma((10,)), dma((5,)), *[dma((2, 2, 4))] * 2, *[dma((2, 2, 2))] * 4,
+            dma((13,)), dma((5,)), *[dma((2, 2, 4))] * 2, *[dma((2, 2, 2))] * 4,
             dma((2, ngx * ngy)), dma((2, ngx * ngy)), pltpu.SemaphoreType.REGULAR,
         ],
         compiler_params=pltpu.CompilerParams(
@@ -646,19 +664,17 @@
     seeds = make_seeds(nx, ny)
     far, e, h, p = pl.pallas_call(
         functools.partial(far_kernel, ngx, ngy, nx, ny),
-        grid=(steps,),
         out_shape=(jax.ShapeDtypeStruct((2, 2, 4, NDIR), F32), field, field, field),
-        in_specs=[
-            pl.BlockSpec(g.shape, lambda i: (0, 0, 0, 0)),
-            pl.BlockSpec((1, *seeds.shape[1:]), lambda i: (i, 0, 0)),
-            hbm, hbm, hbm,
-        ],
-        out_specs=(pl.BlockSpec((2, 2, 4, 4 * TILE), lambda i: (0, 0, 0, i)), hbm, hbm, hbm),
+        in_specs=[hbm] * 5,
+        out_specs=(hbm,) * 4,
         scratch_shapes=[
+            pltpu.VMEM(g.shape, F32),
+            pltpu.VMEM(seeds.shape, F32),
+            pltpu.VMEM((steps, 2, 2, 4, 4 * TILE), F32),
             pltpu.VMEM((2, 2 * width, ny // 2), BF16),
             pltpu.VMEM((2, 2 * width, ny // 2), BF16),
             *[pltpu.VMEM(e_field.shape, F32)] * 3,
-            dma((2, 3)),
+            dma((2, 3)), dma((steps,)), dma((steps,)), dma,
         ],
         compiler_params=pltpu.CompilerParams(vmem_limit_bytes=56 * 1024 * 1024),
     )(g, jnp.asarray(seeds), e, h, p)

time: 35.8 us -> 35 us (0.978)
  Pallas kernels: 34.3 us -> 33.6 us
    pallas_call x1, Pallas kernels: 8.68 us -> 8.3 us  [shards(): pl.pallas_call(functools.partial(far_kernel, ngx, ngy, nx, ny), out_shape...]
where the time goes in v4:
time: 35 us; the launch traced here: 34.9 us
  Pallas kernels  33.6 us (96%)
  between operations  1.29 us (4%)
    pallas_call x1, Pallas kernels, shards(): pl.pallas_call(functools.partial(step_kernel, ngx, ngy, eps_table.shape[0...  25.3 us
    pallas_call x1, Pallas kernels, shards(): pl.pallas_call(functools.partial(far_kernel, ngx, ngy, nx, ny), out_shape...  8.3 us

profile of v4, /device:TPU:0, one launch (start us, length us, event | category | flops | bytes accessed | tf_op | source)
XLA Modules:
  0.0 34.9 jit_solution(8959961782378545097)
XLA Ops:
  1.3 25.3 %shard_map.138 = (f32[3,8,32,512]{3,2,1,0:T(8,128)}, f32[3,8,32,512]{3,2,1,0:T(8,128)}, f32[3,8,32,512]{3,2,1,0:T(8,128)}, f32[2,32,8,128]{3,2,1,0:T(8,128)}) custom-call(f32[3,8,32,512]{3,2,1,0:T(8,128)} %e_in.1, f32[3,8,32,512]{3,2,1,0:T(8,128)} %h_in.1, f32[3,8,32,512]{3,2,1,0:T(8,128)} %p_in.1, f32[3,8,32,512]{3,2,1,0:T(8,128)} %q_in.1, ...), custom_call_target="tpu_custom_call" | custom-call | tf_op jit(solution)/shard_map/pallas_call | solution.py:636
  26.6 8.3 %shard_map.139 = (f32[2,2,4,16384]{3,2,1,0:T(4,128)}, f32[3,8,32,512]{3,2,1,0:T(8,128)}, f32[3,8,32,512]{3,2,1,0:T(8,128)}, f32[3,8,32,512]{3,2,1,0:T(8,128)}) custom-call(f32[2,32,8,128]{3,2,1,0:T(8,128)} %get-tuple-element.12.g_in, f32[4,64,1024]{2,1,0:T(8,128)} %constant.2.clone.seeds_in, f32[3,8,32,512]{3,2,1,0:T(8,128)} %get-tuple-element.13.e_in, ...), custom_call_target="tpu_custom_call" | custom-call | tf_op jit(solution)/shard_map/pallas_call | solution.py:665

commit v5 on v4

--- a/solution.py
+++ b/solution.py
@@ -431,7 +431,7 @@
         save.wait()
 
 
-TILE = 1024
+TILE = 2048
 PART = 256
 
 
@@ -475,9 +475,10 @@
     def seed_load(tile):
         return pltpu.make_async_copy(seeds_in.at[tile], seeds.at[tile], seed_sem.at[tile])
 
-    def far_save(tile):
-        lanes = pl.ds(pl.multiple_of(tile * 4 * TILE, 4 * TILE), 4 * TILE)
-        return pltpu.make_async_copy(far.at[tile], far_out.at[:, :, :, lanes], far_sem.at[tile])
+    def far_save(tile, i):
+        lanes = pl.ds(pl.multiple_of(tile * 4 * TILE + i * 2 * TILE, 2 * TILE), 2 * TILE)
+        src = far.at[tile, :, :, :, pl.ds(i * 2 * TILE, 2 * TILE)]
+        return pltpu.make_async_copy(src, far_out.at[:, :, :, lanes], far_sem.at[tile, i])
 
     for tile in range(tiles):
         seed_load(tile).start()
@@ -533,7 +534,7 @@
             for load, _ in moves:
                 load.start()
 
-        @pl.when(tile == 2)
+        @pl.when(tile == 1)
         def _():
             for load, save in moves:
                 load.wait()
@@ -541,6 +542,8 @@
 
         for o in range(0, TILE, PART):
             lanes = slice(o, o + PART)
+            if o == TILE // 2:
+                far_save(tile, 0).start()
             for f in range(2):
                 omega = 2.0 * math.pi / WAVELENGTHS[f]
                 kappa = [math.cos(omega * (s + 1) * DT) * scale for s in range(2)]
@@ -612,11 +615,12 @@
                             d = (2 * (o // 128 + pair) + t) * 256 + h * 128
                             far[tile, f, 0, :, d : d + 128] = both[t][0:4]
                             far[tile, f, 1, :, d : d + 128] = both[t][4:8]
-        far_save(tile).start()
+        far_save(tile, 1).start()
 
     @pl.loop(0, tiles)
     def _(tile):
-        far_save(tile).wait()
+        far_save(tile, 0).wait()
+        far_save(tile, 1).wait()
 
     for _, save in moves:
         save.wait()
@@ -674,7 +678,7 @@
             pltpu.VMEM((2, 2 * width, ny // 2), BF16),
             pltpu.VMEM((2, 2 * width, ny // 2), BF16),
             *[pltpu.VMEM(e_field.shape, F32)] * 3,
-            dma((2, 3)), dma((steps,)), dma((steps,)), dma,
+            dma((2, 3)), dma((steps,)), dma((steps, 2)), dma,
         ],
         compiler_params=pltpu.CompilerParams(vmem_limit_bytes=56 * 1024 * 1024),
     )(g, jnp.asarray(seeds), e, h, p)

time: 35 us -> 34.3 us (0.980)
  Pallas kernels: 33.6 us -> 32.8 us
    pallas_call x1, Pallas kernels: 8.3 us -> 7.54 us  [shards(): pl.pallas_call(functools.partial(far_kernel, ngx, ngy, nx, ny), out_shape...]
where the time goes in v5:
time: 34.3 us; the launch traced here: 34.1 us
  Pallas kernels  32.8 us (96%)
  between operations  1.29 us (4%)
    pallas_call x1, Pallas kernels, shards(): pl.pallas_call(functools.partial(step_kernel, ngx, ngy, eps_table.shape[0...  25.3 us
    pallas_call x1, Pallas kernels, shards(): pl.pallas_call(functools.partial(far_kernel, ngx, ngy, nx, ny), out_shape...  7.54 us

profile of v5, /device:TPU:0, one launch (start us, length us, event | category | flops | bytes accessed | tf_op | source)
XLA Modules:
  0.0 34.1 jit_solution(16598811757923545354)
XLA Ops:
  1.3 25.3 %shard_map.138 = (f32[3,8,32,512]{3,2,1,0:T(8,128)}, f32[3,8,32,512]{3,2,1,0:T(8,128)}, f32[3,8,32,512]{3,2,1,0:T(8,128)}, f32[2,32,8,128]{3,2,1,0:T(8,128)}) custom-call(f32[3,8,32,512]{3,2,1,0:T(8,128)} %e_in.1, f32[3,8,32,512]{3,2,1,0:T(8,128)} %h_in.1, f32[3,8,32,512]{3,2,1,0:T(8,128)} %p_in.1, f32[3,8,32,512]{3,2,1,0:T(8,128)} %q_in.1, ...), custom_call_target="tpu_custom_call" | custom-call | tf_op jit(solution)/shard_map/pallas_call | solution.py:640
  26.6 7.5 %shard_map.139 = (f32[2,2,4,16384]{3,2,1,0:T(4,128)}, f32[3,8,32,512]{3,2,1,0:T(8,128)}, f32[3,8,32,512]{3,2,1,0:T(8,128)}, f32[3,8,32,512]{3,2,1,0:T(8,128)}) custom-call(f32[2,32,8,128]{3,2,1,0:T(8,128)} %get-tuple-element.12.g_in, f32[2,64,2048]{2,1,0:T(8,128)} %constant.2.clone.seeds_in, f32[3,8,32,512]{3,2,1,0:T(8,128)} %get-tuple-element.13.e_in, ...), custom_call_target="tpu_custom_call" | custom-call | tf_op jit(solution)/shard_map/pallas_call | solution.py:669

commit v6 on v5

--- a/solution.py
+++ b/solution.py
@@ -99,15 +99,11 @@
 
     def x_copies(step, way, part):
         lanes = lanes_of(step, way, part)
-        copies = []
-        for i in range(2):
-            src = E.at[1 + i, 0, :, lanes] if way == 0 else xstage.at[step, i, :, lanes]
-            dst = (xe, xh)[way].at[step, i, :, lanes]
-            copies.append(pltpu.make_async_remote_copy(
-                src_ref=src, dst_ref=dst,
-                send_sem=xs_sem.at[step, way, 2 * part + i], recv_sem=xr_sem.at[step, way, 2 * part + i],
-                device_id=(lax.rem(gx + (ngx - 1, 1)[way], ngx), gy), device_id_type=MESH))
-        return copies
+        src = E.at[pl.ds(1, 2), 0, :, lanes] if way == 0 else xstage.at[step, :, :, lanes]
+        return [pltpu.make_async_remote_copy(
+            src_ref=src, dst_ref=(xe, xh)[way].at[step, :, :, lanes],
+            send_sem=xs_sem.at[step, way, part], recv_sem=xr_sem.at[step, way, part],
+            device_id=(lax.rem(gx + (ngx - 1, 1)[way], ngx), gy), device_id_type=MESH)]
 
     def y_copy(step, way, part):
         lanes = lanes_of(step, way, part)

time: 34.3 us -> 34.2 us (level)
  no operation moved by 1% of the time
where the time goes in v6:
time: 34.2 us; the launch traced here: 34.1 us
  Pallas kernels  32.8 us (96%)
  between operations  1.29 us (4%)
    pallas_call x1, Pallas kernels, shards(): pl.pallas_call(functools.partial(step_kernel, ngx, ngy, eps_table.shape[0...  25.3 us
    pallas_call x1, Pallas kernels, shards(): pl.pallas_call(functools.partial(far_kernel, ngx, ngy, nx, ny), out_shape...  7.52 us

profile of v6, /device:TPU:0, one launch (start us, length us, event | category | flops | bytes accessed | tf_op | source)
XLA Modules:
  0.0 34.1 jit_solution(9225273415360877269)
XLA Ops:
  1.3 25.3 %shard_map.138 = (f32[3,8,32,512]{3,2,1,0:T(8,128)}, f32[3,8,32,512]{3,2,1,0:T(8,128)}, f32[3,8,32,512]{3,2,1,0:T(8,128)}, f32[2,32,8,128]{3,2,1,0:T(8,128)}) custom-call(f32[3,8,32,512]{3,2,1,0:T(8,128)} %e_in.1, f32[3,8,32,512]{3,2,1,0:T(8,128)} %h_in.1, f32[3,8,32,512]{3,2,1,0:T(8,128)} %p_in.1, f32[3,8,32,512]{3,2,1,0:T(8,128)} %q_in.1, ...), custom_call_target="tpu_custom_call" | custom-call | tf_op jit(solution)/shard_map/pallas_call | solution.py:636
  26.6 7.5 %shard_map.139 = (f32[2,2,4,16384]{3,2,1,0:T(4,128)}, f32[3,8,32,512]{3,2,1,0:T(8,128)}, f32[3,8,32,512]{3,2,1,0:T(8,128)}, f32[3,8,32,512]{3,2,1,0:T(8,128)}) custom-call(f32[2,32,8,128]{3,2,1,0:T(8,128)} %get-tuple-element.12.g_in, f32[2,64,2048]{2,1,0:T(8,128)} %constant.2.clone.seeds_in, f32[3,8,32,512]{3,2,1,0:T(8,128)} %get-tuple-element.13.e_in, ...), custom_call_target="tpu_custom_call" | custom-call | tf_op jit(solution)/shard_map/pallas_call | solution.py:665
